TPU v7x, 128 devices: a whole 4x4x4 slice. The times are simulated.
128 devices in a mesh: section: 8 (over z, y_hi), dp: 16 (over x, y_lo, core).
Axes of the slice: x: 4, y: 4 (y_hi: 2, y_lo: 2; y = y_hi * 2 + y_lo), z: 4, core: 2. Of those that a mesh axis runs over, the one named last changes fastest.
Arguments:
- incoming: bfloat16 [8, 1024, 4096], P('section', 'dp'), may hold values from -6 to 6
- parked: bfloat16 [8, 1024, 4096], P('section', 'dp'), may hold values from -6 to 6
- cotangent: bfloat16 [8, 1024, 4096], P('section', 'dp'), may hold values from -6 to 6
- norm_gain: float32 [8, 4096], P('section'), may hold values from 0.5 to 1.5
- query_weight: bfloat16 [8, 4096, 4096], P('section', None, 'dp'), may hold values from -2.90625 to 2.90625
- keyval_weight: bfloat16 [8, 4096, 2048], P('section', None, 'dp'), may hold values from -0.09375 to 0.09375
- output_weight: bfloat16 [8, 4096, 4096], P('section', 'dp'), may hold values from -0.09375 to 0.09375
- teacher_id: int32 [1024], P('dp'), may hold values from 0 to 3
- language_id: int32 [1024], P('dp'), may hold values from 0 to 15
Outputs:
- next_input: bfloat16 [8, 1024, 4096], P('section', 'dp')
- input_grad: bfloat16 [8, 1024, 4096], P('section', 'dp')
- parked_next: bfloat16 [8, 1024, 4096], P('section', 'dp')
- query_grad: bfloat16 [8, 4096, 4096], P('section', None, 'dp')
- keyval_grad: bfloat16 [8, 4096, 2048], P('section', None, 'dp')
- output_grad: bfloat16 [8, 4096, 4096], P('section', 'dp')
- gain_grad: float32 [8, 4096], P('section', 'dp')
All inputs are finite; a program needn't handle non-finite values.
Results may differ from a plain program's by a relative error of at most 0.024.
Values may be sent and summed in bfloat16 or wider, within the bound.
A program may use at most 192 MiB of HBM per device.

v0:
```python
import math

import jax
import jax.numpy as jnp
from jax import lax
from jax.sharding import PartitionSpec as P

LANGS = 16


EPSILON = 1e-05
NEG_FILL = -1e30


def from_partner(value, axis, bit):
    mask = 2**bit
    pairs = [(source, source ^ mask) for source in range(lax.axis_size(axis))]
    return lax.ppermute(value, axis, pairs)


def passed_along(value, axis, steps):
    count = lax.axis_size(axis)
    pairs = [(source, (source + steps) % count) for source in range(count)]
    return lax.ppermute(value, axis, pairs)


def normalize(row_block, gain_row):
    values = row_block.astype(jnp.float32)
    inverse_rms = lax.rsqrt(jnp.mean(values * values, axis=-1, keepdims=True) + EPSILON)
    return values * inverse_rms * gain_row


def attend(queries, key_rows, values):
    length = queries.shape[0]
    scores = jnp.einsum("qhd,kd->hqk", queries, key_rows, precision=lax.Precision.HIGHEST) * (
        1.0 / math.sqrt(key_rows.shape[-1])
    )
    row_index = lax.broadcasted_iota(jnp.int32, (length, length), 0)
    col_index = lax.broadcasted_iota(jnp.int32, (length, length), 1)
    scores = jnp.where((col_index <= row_index)[None], scores, NEG_FILL)
    row_max = lax.stop_gradient(jnp.max(scores, axis=-1, keepdims=True))
    weights = jnp.exp(scores - row_max)
    weights = weights / jnp.sum(weights, axis=-1, keepdims=True)
    return jnp.einsum("hqk,kd->qhd", weights, values, precision=lax.Precision.HIGHEST)


def body(
    incoming,
    parked,
    cotangent,
    norm_gain,
    query_weight,
    keyval_weight,
    output_weight,
    teacher_id,
    language_id,
):
    sections = lax.axis_size("section")
    section_rank = lax.axis_index("section")
    data_rank = lax.axis_index("dp")
    is_even = data_rank % 2 == 0
    gain_row = norm_gain[0]
    weight_query = query_weight[0]
    weight_keyval = keyval_weight[0]
    weight_output = output_weight[0]
    head_dim = weight_keyval.shape[1]
    head_width = weight_query.shape[1]
    heads_here = head_width // head_dim

    def project(row_piece):
        query_part = jnp.dot(row_piece, weight_query, preferred_element_type=jnp.float32)
        keyval_part = jnp.dot(row_piece, weight_keyval, preferred_element_type=jnp.float32)
        return jnp.concatenate([query_part, keyval_part], axis=1).astype(jnp.bfloat16)

    def split_heads(combined):
        length = combined.shape[0]
        queries = combined[:, :head_width].astype(jnp.float32).reshape(length, heads_here, head_dim)
        own_part = combined[:, head_width:]
        partner = from_partner(own_part, "dp", 0)
        key_rows = jnp.where(is_even, own_part, partner).astype(jnp.float32)
        values = jnp.where(is_even, partner, own_part).astype(jnp.float32)
        return (queries, key_rows, values)

    parked_next = passed_along(incoming, "section", sections // 2)
    normed = normalize(incoming[0], gain_row).astype(jnp.bfloat16)
    combined = project(lax.all_gather(normed, "dp", axis=0, tiled=True))
    length = combined.shape[0]
    queries, key_rows, values = split_heads(combined)
    attended = attend(queries, key_rows, values).reshape(length, head_width).astype(jnp.bfloat16)
    summed = lax.psum_scatter(
        jnp.dot(attended, weight_output, preferred_element_type=jnp.float32).astype(jnp.bfloat16),
        "dp",
        scatter_dimension=0,
        tiled=True,
    ).astype(jnp.float32)
    result = (incoming[0].astype(jnp.float32) + summed).astype(jnp.bfloat16)
    next_input = passed_along(result[None], "section", 1)
    stash_rows = passed_along(parked, "section", sections // 2)[0]
    token_weight = jnp.power(0.5, teacher_id.astype(jnp.float32)) * (
        0.5 + language_id.astype(jnp.float32) / (LANGS - 1)
    )
    scaled = (cotangent[0].astype(jnp.float32) * token_weight[:, None]).astype(jnp.bfloat16)
    upstream = jnp.where(section_rank == sections - 1, scaled, cotangent[0])
    normed_f, undo_norm = jax.vjp(normalize, stash_rows.astype(jnp.float32), gain_row)
    normed = normed_f.astype(jnp.bfloat16)
    normed_all = lax.all_gather(normed, "dp", axis=0, tiled=True)
    upstream_all = lax.all_gather(upstream, "dp", axis=0, tiled=True)
    combined = project(normed_all)
    length = combined.shape[0]
    queries, key_rows, values = split_heads(combined)
    attended_f, undo_attend = jax.vjp(attend, queries, key_rows, values)
    backward_attended = attended_f.reshape(length, head_width).astype(jnp.bfloat16)
    out_grad = jnp.einsum(
        "ta,td->ad", backward_attended, upstream_all, preferred_element_type=jnp.float32
    ).astype(jnp.bfloat16)
    d_attended = jnp.einsum(
        "td,ad->ta", upstream_all, weight_output, preferred_element_type=jnp.float32
    )
    d_heads, d_keys, d_values = undo_attend(d_attended.reshape(length, heads_here, head_dim))
    d_queries = d_heads.reshape(length, head_width).astype(jnp.bfloat16)
    kept_part = jnp.where(is_even, d_keys, d_values)
    sent_part = jnp.where(is_even, d_values, d_keys)
    d_keyval = (
        kept_part + from_partner(sent_part.astype(jnp.bfloat16), "dp", 0).astype(sent_part.dtype)
    ).astype(jnp.bfloat16)
    query_part = jnp.einsum(
        "tc,ta->ca", normed_all, d_queries, preferred_element_type=jnp.float32
    ).astype(jnp.bfloat16)
    keyval_part = jnp.einsum(
        "tc,ta->ca", normed_all, d_keyval, preferred_element_type=jnp.float32
    ).astype(jnp.bfloat16)
    first = jnp.einsum("ta,ca->tc", d_queries, weight_query, preferred_element_type=jnp.float32)
    d_normed = lax.psum_scatter(
        (
            first
            + jnp.einsum("ta,ca->tc", d_keyval, weight_keyval, preferred_element_type=jnp.float32)
        ).astype(jnp.bfloat16),
        "dp",
        scatter_dimension=0,
        tiled=True,
    ).astype(jnp.float32)
    d_rows, d_gain = undo_norm(d_normed)
    gain_part = lax.psum_scatter(d_gain, "dp", scatter_dimension=0, tiled=True)
    back_rows = (upstream.astype(jnp.float32) + d_rows).astype(jnp.bfloat16)
    passed = passed_along(back_rows[None], "section", -1)
    query_grad = query_part[None]
    keyval_grad = keyval_part[None]
    output_grad = out_grad[None]
    gain_grad = gain_part[None]
    return (next_input, passed, parked_next, query_grad, keyval_grad, output_grad, gain_grad)


def solution(mesh):
    return jax.shard_map(
        body,
        mesh=mesh,
        in_specs=(
            P("section", "dp", None),
            P("section", "dp", None),
            P("section", "dp", None),
            P("section", None),
            P("section", None, "dp"),
            P("section", None, "dp"),
            P("section", "dp", None),
            P("dp"),
            P("dp"),
        ),
        out_specs=(
            P("section", "dp", None),
            P("section", "dp", None),
            P("section", "dp", None),
            P("section", None, "dp"),
            P("section", None, "dp"),
            P("section", "dp", None),
            P("section", "dp"),
        ),
        check_vma=False,
    )
```

profile of v0, /device:TPU:1, one launch (start us, length us, event | category | flops | bytes accessed | tf_op | source)
XLA Modules:
  0.0 501.2 jit_solution(9558581019645124161)
XLA Ops:
  7.2 0.8 add_multiply_fusion
  8.1 2.1 fusion.57
  10.2 4.5 collective-permute-start.2
  14.7 1.2 fusion.46
  15.9 10.6 %collective-permute-done.2 = bf16[1,64,4096]{2,1,0:T(8,128)(2,1)S(1)} collective-permute-done((bf16[1,64,4096]{2,1,0:T(8,128)(2,1)}, bf16[1,64,4096]{2,1,0:T(8,128)(2,1)S(1)}, u32[]{:S(2)}, u32[]{:S(2)}) %collective-permute-start.2) | collective-permute-done | bytes 524320 | tf_op jit(solution)/shard_map/ppermute | solution.py:24
  26.8 2.4 fusion.42
  29.2 0.7 all-gather.8.cloned.1.call-update
  30.0 1.3 iota_compare_fusion.1
  31.2 34.8 %all-gather.6.cloned.1.call-done = bf16[1024,4096]{1,0:T(8,128)(2,1)} async-done(((bf16[64,4096]{1,0:T(8,128)(2,1)}), bf16[1024,4096]{1,0:T(8,128)(2,1)}) %all-gather.6.cloned.1.call-update) | async-done | bytes 8388624 | tf_op jit(solution)/shard_map/all_gather | solution.py:107
  66.1 5.8 %fusion.28 = f32[128,2,1024]{0,2,1:T(8,128)} fusion(bf16[2,128,4096]{2,1,0:T(8,128)(2,1)S(1)} %bitcast.157, bf16[1024,4096]{1,0:T(8,128)(2,1)} %all-gather.6.cloned.1.call-done), kind=kOutput, calls=%fused_computation.49 | convolution fusion | flops 2147483648 | bytes 11534336 | tf_op jit(solution)/shard_map/td,ad->ta/dot_general | solution.py:116
  71.8 49.5 %all-gather.4.cloned.1.call-done = bf16[1024,4096]{1,0:T(8,128)(2,1)} async-done(((bf16[64,4096]{1,0:T(8,128)(2,1)}), bf16[1024,4096]{1,0:T(8,128)(2,1)}) %all-gather.4.cloned.1.call-update) | async-done | bytes 8388624 | tf_op jit(solution)/shard_map/all_gather | solution.py:86
  121.3 6.6 %convolution_convert_fusion.7 = bf16[1024,128]{1,0:T(8,128)(2,1)} fusion(bf16[1024,4096]{1,0:T(8,128)(2,1)} %all-gather.4.cloned.1.call-done, bf16[1,4096,128]{2,1,0:T(8,128)(2,1)} %param.14), kind=kOutput, calls=%fused_computation.62 | convolution fusion | flops 1073872896 | bytes 9699328 | tf_op jit(solution)/shard_map/dot_general | solution.py:72
  128.2 48.4 %all-gather.8.cloned.1.call-done = bf16[1024,4096]{1,0:T(8,128)(2,1)} async-done(((bf16[64,4096]{1,0:T(8,128)(2,1)}), bf16[1024,4096]{1,0:T(8,128)(2,1)}) %all-gather.8.cloned.1.call-update) | async-done | bytes 8388624 | tf_op jit(solution)/shard_map/all_gather | solution.py:106
  176.6 6.1 %convolution_convert_fusion.6 = bf16[1024,128]{1,0:T(8,128)(2,1)S(1)} fusion(bf16[1024,4096]{1,0:T(8,128)(2,1)} %all-gather.8.cloned.1.call-done, bf16[1,4096,128]{2,1,0:T(8,128)(2,1)} %param.14), kind=kOutput, calls=%fused_computation.61 | convolution fusion | flops 1073872896 | bytes 9699328 | tf_op jit(solution)/shard_map/dot_general | solution.py:72
  182.7 0.6 collective-permute-start.3
  183.3 6.2 %fusion.31 = bf16[1024,256]{0,1:T(8,128)(2,1)S(1)} fusion(bf16[1024,4096]{1,0:T(8,128)(2,1)} %all-gather.4.cloned.1.call-done, bf16[1,4096,256]{2,1,0:T(8,128)(2,1)S(1)} %copy-done.5), kind=kOutput, calls=%fused_computation.52 | convolution fusion | flops 2147745792 | bytes 11010048 | tf_op jit(solution)/shard_map/dot_general | solution.py:71
  189.5 2.4 fusion.34
  192.0 1.9 fusion.8
  193.9 8.0 %fusion.15 = (f32[2,1024]{1,0:T(2,128)S(1)}, f32[2,1024]{1,0:T(2,128)S(1)}, f32[1024,1024,2]{1,0,2:T(8,128)}) fusion(f32[1024,1024,2]{1,0,2:T(8,128)S(1)} %get-tuple-element.16, f32[2,1024]{1,0:T(2,128)S(1)} %get-tuple-element.15, pred[1024,1024]{0,1:T(8,128)(4,1)S(1)} %copy-done.8, bf16[1024,2,128]{0,2,1:T(8,128)(2,1)S(1)} %bitcast.175, ...), kind=kOutput, calls=%fused_computation.26 | convolution fusion | flops 551677952 | bytes 18898944 | tf_op jit(solution)/shard_map/qhd,kd->hqk/dot_general | solution.py:35
  201.9 12.4 %multiply_reduce_fusion = (f32[2,1024]{1,0:T(2,128)S(1)}, f32[2,1024]{1,0:T(2,128)S(1)}, f32[2,1024,1024]{1,2,0:T(8,128)}) fusion(f32[1024,1024,2]{1,0,2:T(8,128)S(1)} %get-tuple-element.16, f32[2,1024]{1,0:T(2,128)S(1)} %multiply_divide_fusion, f32[2,1024]{1,0:T(2,128)S(1)} %get-tuple-element.15, pred[1024,1024]{0,1:T(8,128)(4,1)S(1)} %copy-done.8, ...), kind=kOutput, calls=%fused_computation.10 | convolution fusion | flops 3242323968 | bytes 27828224 | tf_op jit(solution)/shard_map/transpose(jvp(hqk,kd->qhd))/dot_general | solution.py:44
  214.4 6.5 %fusion.37 = bf16[128,2,1024]{2,0,1:T(8,128)(2,1)S(1)} fusion(f32[1024,1024,2]{1,0,2:T(8,128)S(1)} %copy-done.19, f32[2,1024]{1,0:T(2,128)S(1)} %get-tuple-element.10, f32[2,1024]{1,0:T(2,128)S(1)} %get-tuple-element.12, pred[1024,1024]{0,1:T(8,128)(4,1)S(1)} %copy-done.8, bf16[1024,128]{1,0:T(8,128)(2,1)} %collective-permute-done, ...), kind=kOutput, calls=%fused_computation.54 | convolution fusion | flops 3230007296 | bytes 10502145 | tf_op jit(solution)/shard_map/hqk,kd->qhd/dot_general | solution.py:44
  220.9 5.6 %convolution_convert_fusion = bf16[1024,4096]{1,0:T(8,128)(2,1)} fusion(bf16[1024,256]{0,1:T(8,128)(2,1)S(1)} %bitcast.164, bf16[1,256,4096]{2,1,0:T(8,128)(2,1)S(1)} %copy-done), kind=kOutput, calls=%fused_computation.16 | convolution fusion | flops 2151677952 | bytes 11010048 | tf_op jit(solution)/shard_map/dot_general | solution.py:91
  227.0 7.8 %fusion.3 = f32[1024,1024,2]{1,0,2:T(8,128)S(1)} fusion(f32[2,1024,1024]{1,2,0:T(8,128)} %get-tuple-element.18, f32[1024,1024,2]{1,0,2:T(8,128)} %copy-done.2, f32[1024,2]{0,1:T(2,128)S(1)} %bitcast.169, f32[1024,2]{0,1:T(2,128)S(1)} %negate_bitcast_fusion, f32[1024,2]{0,1:T(2,128)S(1)} %bitcast.168, pred[1024,1024]{1,0:T(8,128)(4,1)S(1)} %iota_compare_fusion), kind=kLoop, calls=%fused_computation.6 | loop fusion | flops 16777216 | bytes 26238976 | tf_op jit(solution)/shard_map/transpose(jvp())/mul | solution.py:35
  234.8 3.9 convolution_bitcast_fusion.1
  238.7 8.5 %select_convert_fusion = (bf16[1024,128]{1,0:T(8,128)(2,1)S(1)}, f32[1024,128]{1,0:T(8,128)S(1)}) fusion(f32[1024,128]{1,0:T(8,128)S(1)} %convolution_bitcast_fusion.1, pred[]{:T(512)S(6)} %eq.8, f32[128,2,1024]{0,2,1:T(8,128)S(1)} %copy-done.21, f32[1024,1024,2]{1,0,2:T(8,128)S(1)} %bitcast.159, f32[2,1024]{1,0:T(2,128)S(1)} %get-tuple-element.11, ...), kind=kOutput, calls=%fused_computation.81 | convolution fusion | flops 3229745152 | bytes 11812865 | tf_op jit(solution)/shard_map/transpose(jvp(hqk,kd->qhd))/dot_general | solution.py:44
  247.6 3.1 convolution_convert_fusion.5
  250.8 8.2 %fusion.22 = f32[1024,4096]{1,0:T(8,128)} fusion(bf16[1024,256]{0,1:T(8,128)(2,1)S(1)} %bitcast.160, bf16[1,4096,256]{2,1,0:T(8,128)(2,1)S(1)} %copy-done.6), kind=kOutput, calls=%fused_computation.35 | convolution fusion | flops 2147483648 | bytes 19398656 | tf_op jit(solution)/shard_map/ta,ca->tc/dot_general | solution.py:132
  259.1 11.6 %add_convert_fusion = bf16[1024,4096]{1,0:T(8,128)(2,1)} fusion(f32[1024,4096]{1,0:T(8,128)} %fusion.22, bf16[1024,128]{1,0:T(8,128)(2,1)S(1)} %add_convert_fusion.1, bf16[1,4096,128]{2,1,0:T(8,128)(2,1)S(1)} %copy-done.7), kind=kOutput, calls=%fused_computation | convolution fusion | flops 1082130432 | bytes 26476544 | tf_op jit(solution)/shard_map/ta,ca->tc/dot_general | solution.py:136
  270.7 1.0 copy-done.3
  271.8 3.1 collective-permute-start.6
  274.9 0.6 dynamic-slice
  276.1 10.8 %collective-permute-done.6 = bf16[1,64,4096]{2,1,0:T(8,128)(2,1)S(1)} collective-permute-done((bf16[1,64,4096]{2,1,0:T(8,128)(2,1)S(1)}, bf16[1,64,4096]{2,1,0:T(8,128)(2,1)S(1)}, u32[]{:S(2)}, u32[]{:S(2)}) %collective-permute-start.6) | collective-permute-done | bytes 524320 | tf_op jit(solution)/shard_map/ppermute | solution.py:24
  286.9 7.5 %fusion.11 = bf16[1,4096,256]{2,1,0:T(8,128)(2,1)} fusion(bf16[1024,4096]{1,0:T(8,128)(2,1)} %all-gather.8.cloned.1.call-done, bf16[1024,256]{0,1:T(8,128)(2,1)S(1)} %bitcast.161), kind=kOutput, calls=%fused_computation.21 | convolution fusion | flops 2148532224 | bytes 11010048 | tf_op jit(solution)/shard_map/tc,ta->ca/dot_general | solution.py:126
  294.5 9.0 %convolution_convert_fusion.4 = bf16[128,2,1024]{2,0,1:T(8,128)(2,1)S(1)} fusion(f32[1024,1024,2]{1,0,2:T(8,128)} %copy-done.2, f32[2,1024]{1,0:T(2,128)S(1)} %get-tuple-element.11, f32[2,1024]{1,0:T(2,128)S(1)} %get-tuple-element.15, pred[1024,1024]{0,1:T(8,128)(4,1)S(1)} %copy-done.10, bf16[1024,128]{1,0:T(8,128)(2,1)S(1)} %copy-done.16, ...), kind=kOutput, calls=%fused_computation.55 | convolution fusion | flops 3230007296 | bytes 10502145 | tf_op jit(solution)/shard_map/jvp(hqk,kd->qhd)/dot_general | solution.py:44
  303.6 3.7 fusion.12
  307.3 16.8 %reduce-scatter.3.cloned.1.call-done = bf16[64,4096]{1,0:T(8,128)(2,1)} async-done(((bf16[1024,4096]{1,0:T(8,128)(2,1)}), bf16[64,4096]{1,0:T(8,128)(2,1)}) %reduce-scatter.3.cloned.1.call-update) | async-done | bytes 524304 | tf_op jit(solution)/shard_map/reduce_scatter | solution.py:90
  324.1 2.0 fusion.58
  326.0 1.9 collective-permute-start.1
  327.9 98.8 %reduce-scatter.5.cloned.1.call-done = bf16[64,4096]{1,0:T(8,128)(2,1)} async-done(((bf16[1024,4096]{1,0:T(8,128)(2,1)}), bf16[64,4096]{1,0:T(8,128)(2,1)}) %reduce-scatter.5.cloned.1.call-update) | async-done | bytes 524304 | tf_op jit(solution)/shard_map/reduce_scatter | solution.py:133
  426.7 1.5 fusion.43
  428.2 2.4 fusion.59
  430.6 2.8 collective-permute-start.5
  433.4 6.8 %fusion.13 = bf16[1,4096,128]{2,1,0:T(8,128)(2,1)} fusion(bf16[1024,4096]{1,0:T(8,128)(2,1)} %all-gather.8.cloned.1.call-done, bf16[1024,128]{1,0:T(8,128)(2,1)S(1)} %add_convert_fusion.1), kind=kOutput, calls=%fused_computation.24 | convolution fusion | flops 1074266112 | bytes 9699328 | tf_op jit(solution)/shard_map/tc,ta->ca/dot_general | solution.py:129
  440.2 49.2 %all-reduce = f32[4096]{0:T(1024)S(1)} all-reduce(f32[4096]{0:T(1024)S(1)} %get-tuple-element.7), channel_id=4, replica_groups=mesh['section'=8,'dp'=16] {'dp'}, use_global_device_ids=true, to_apply=%region_11.12.clone | all-reduce | flops 4096 | bytes 32768
  489.3 0.6 dynamic-slice.1
  490.0 1.9 copy.52
  491.8 0.8 copy.53
  492.6 1.9 copy.54
  (82 shorter events, 1.7 us)
Async XLA Ops:
  7.2 58.9 %copy-start = (bf16[1,256,4096]{2,1,0:T(8,128)(2,1)S(1)}, bf16[1,256,4096]{2,1,0:T(8,128)(2,1)}, u32[]{:S(2)}) copy-start(bf16[1,256,4096]{2,1,0:T(8,128)(2,1)} %param.15) | copy-start | bytes 6291460
  7.2 58.9 %all-gather.6.cloned.1.call-start = ((), (), s32[]{:S(2)}) async-start(), calls=%async_computation.4 | async-start | bytes 8912896 | tf_op jit(solution)/shard_map/all_gather | solution.py:107
  10.1 111.2 %all-gather.4.cloned.1.call-start = ((), (), s32[]{:S(2)}) async-start(), calls=%async_computation.2 | async-start | bytes 8912896 | tf_op jit(solution)/shard_map/all_gather | solution.py:86
  10.2 16.4 %collective-permute-start.2 = (bf16[1,64,4096]{2,1,0:T(8,128)(2,1)}, bf16[1,64,4096]{2,1,0:T(8,128)(2,1)S(1)}, u32[]{:S(2)}, u32[]{:S(2)}) collective-permute-start(bf16[1,64,4096]{2,1,0:T(8,128)(2,1)} %param.10), channel_id=1, source_target_pairs={{0,64},{16,80},{32,96},{48,112},{64,0},{80,16},{96,32},{112,48},{1... | collective-permute-start | bytes 1572872 | tf_op jit(solution)/shard_map/ppermute | solution.py:24
  29.2 147.5 %all-gather.8.cloned.1.call-start = ((), (), s32[]{:S(2)}) async-start(), calls=%async_computation.5 | async-start | bytes 8912896 | tf_op jit(solution)/shard_map/all_gather | solution.py:106
  29.9 294.2 %reduce-scatter.3.cloned.1.call-start = ((), (), s32[]{:S(2)}) async-start(), calls=%async_computation.3 | async-start | bytes 8912896 | tf_op jit(solution)/shard_map/reduce_scatter | solution.py:90
  128.0 65.9 %collective-permute-start = (bf16[1024,128]{1,0:T(8,128)(2,1)}, bf16[1024,128]{1,0:T(8,128)(2,1)}, u32[]{:S(2)}, u32[]{:S(2)}) collective-permute-start(bf16[1024,128]{1,0:T(8,128)(2,1)} %convolution_convert_fusion.7), channel_id=1, source_target_pairs={{0,1},{1,0},{2,3},{3,2},{4,5},{5,4},{6,7},{7,6},{8,9},{9,8},{10,11... | collective-permute-start | bytes 786440 | tf_op jit(solution)/shard_map/ppermute | solution.py:18
  176.6 6.7 %copy-start.5 = (bf16[1,4096,256]{2,1,0:T(8,128)(2,1)S(1)}, bf16[1,4096,256]{2,1,0:T(8,128)(2,1)}, u32[]{:S(2)}) copy-start(bf16[1,4096,256]{2,1,0:T(8,128)(2,1)} %param.13) | copy-start | bytes 6291460
  176.6 12.9 %slice-start.4 = ((s8[8388608]{0:T(1024)(128)(4,1)}), s8[4194304]{0:T(1024)(128)(4,1)S(1)}, s32[]{:S(2)}) async-start(s8[8388608]{0:T(1024)(128)(4,1)} %bitcast.173), calls=%async_computation.11 | async-start | bytes 8388608
  182.7 64.9 %copy-start.12 = (bf16[1024,128]{1,0:T(8,128)(2,1)}, bf16[1024,128]{1,0:T(8,128)(2,1)S(1)}, u32[]{:S(2)}) copy-start(bf16[1024,128]{1,0:T(8,128)(2,1)S(1)} %convolution_convert_fusion.6) | copy-start | bytes 786436
  182.7 6.8 %slice-start.5 = ((s8[8388608]{0:T(1024)(128)(4,1)}), s8[4194304]{0:T(1024)(128)(4,1)S(1)}, s32[]{:S(2)}) async-start(s8[8388608]{0:T(1024)(128)(4,1)} %bitcast.173), calls=%async_computation.12 | async-start | bytes 8388608
  182.7 9.2 %collective-permute-start.3 = (bf16[1024,128]{1,0:T(8,128)(2,1)S(1)}, bf16[1024,128]{1,0:T(8,128)(2,1)S(1)}, u32[]{:S(2)}, u32[]{:S(2)}) collective-permute-start(bf16[1024,128]{1,0:T(8,128)(2,1)S(1)} %convolution_convert_fusion.6), channel_id=1, source_target_pairs={{0,1},{1,0},{2,3},{3,2},{4,5},{5,4},{6,7},{7,6},{8,9},{9,8},{10,11... | collective-permute-start | bytes 786440 | tf_op jit(solution)/shard_map/ppermute | solution.py:18
  189.5 2.4 copy-start.8
  192.0 9.9 %copy-start.14 = (bf16[1024,128]{1,0:T(8,128)(2,1)}, bf16[1024,128]{1,0:T(8,128)(2,1)S(1)}, u32[]{:S(2)}) copy-start(bf16[1024,128]{1,0:T(8,128)(2,1)S(1)} %collective-permute-done.3) | copy-start | bytes 786436
  193.9 8.0 %copy-start.2 = (f32[1024,1024,2]{1,0,2:T(8,128)}, f32[1024,1024,2]{1,0,2:T(8,128)S(1)}, u32[]{:S(2)}) copy-start(f32[1024,1024,2]{1,0,2:T(8,128)S(1)} %get-tuple-element.16) | copy-start | bytes 25165828
  193.9 8.0 %copy-start.20 = (f32[128,2,1024]{0,2,1:T(8,128)S(1)}, f32[128,2,1024]{0,2,1:T(8,128)}, u32[]{:S(2)}) copy-start(f32[128,2,1024]{0,2,1:T(8,128)} %fusion.28) | copy-start | bytes 3145732
  201.9 12.4 %copy-start.19 = (f32[1024,1024,2]{1,0,2:T(8,128)S(1)}, f32[1024,1024,2]{1,0,2:T(8,128)}, u32[]{:S(2)}) copy-start(f32[1024,1024,2]{1,0,2:T(8,128)} %get-tuple-element.17) | copy-start | bytes 25165828
  226.6 200.1 %reduce-scatter.5.cloned.1.call-start = ((), (), s32[]{:S(2)}) async-start(), calls=%async_computation.6 | async-start | bytes 8912896 | tf_op jit(solution)/shard_map/reduce_scatter | solution.py:133
  226.6 12.0 %slice-start = ((s8[8388608]{0:T(1024)(128)(4,1)}), s8[4194304]{0:T(1024)(128)(4,1)S(1)}, s32[]{:S(2)}) async-start(s8[8388608]{0:T(1024)(128)(4,1)} %bitcast.158), calls=%async_computation.7 | async-start | bytes 8388608
  227.0 11.7 %slice-start.1 = ((s8[8388608]{0:T(1024)(128)(4,1)}), s8[4194304]{0:T(1024)(128)(4,1)S(1)}, s32[]{:S(2)}) async-start(s8[8388608]{0:T(1024)(128)(4,1)} %bitcast.158), calls=%async_computation.8 | async-start | bytes 8388608
  234.7 3.9 copy-start.9
  234.7 3.9 copy-start.21
  238.7 8.9 %copy-start.15 = (bf16[1024,128]{1,0:T(8,128)(2,1)S(1)}, bf16[1024,128]{1,0:T(8,128)(2,1)}, u32[]{:S(2)}) copy-start(bf16[1024,128]{1,0:T(8,128)(2,1)} %copy-done.14) | copy-start | bytes 786436
  247.3 3.5 copy-start.6
  247.3 11.7 %collective-permute-start.4 = (bf16[1024,128]{1,0:T(8,128)(2,1)S(1)}, bf16[1024,128]{1,0:T(8,128)(2,1)S(1)}, u32[]{:S(2)}, u32[]{:S(2)}) collective-permute-start(bf16[1024,128]{1,0:T(8,128)(2,1)S(1)} %get-tuple-element.19), channel_id=1, source_target_pairs={{0,1},{1,0},{2,3},{3,2},{4,5},{5,4},{6,7},{7,6},{8,9},{9,8},{10,11... | collective-permute-start | bytes 786440 | tf_op jit(solution)/shard_map/ppermute | solution.py:18
  250.8 8.3 %copy-start.7 = (bf16[1,4096,128]{2,1,0:T(8,128)(2,1)S(1)}, bf16[1,4096,128]{2,1,0:T(8,128)(2,1)}, u32[]{:S(2)}) copy-start(bf16[1,4096,128]{2,1,0:T(8,128)(2,1)} %param.14) | copy-start | bytes 3145732
  270.7 1.1 copy-start.3
  270.7 4.2 copy-start.18
  271.8 15.2 %collective-permute-start.6 = (bf16[1,64,4096]{2,1,0:T(8,128)(2,1)S(1)}, bf16[1,64,4096]{2,1,0:T(8,128)(2,1)S(1)}, u32[]{:S(2)}, u32[]{:S(2)}) collective-permute-start(bf16[1,64,4096]{2,1,0:T(8,128)(2,1)S(1)} %copy-done.3), channel_id=1, source_target_pairs={{0,64},{16,80},{32,96},{48,112},{64,0},{80,16},{96,32},{112,48},{1... | collective-permute-start | bytes 1572872 | tf_op jit(solution)/shard_map/ppermute | solution.py:24
  276.1 18.4 %copy-start.10 = (pred[1024,1024]{0,1:T(8,128)(4,1)S(1)}, pred[1024,1024]{0,1:T(8,128)(4,1)}, u32[]{:S(2)}) copy-start(pred[1024,1024]{0,1:T(8,128)(4,1)} %iota_compare_fusion.1) | copy-start | bytes 3145732
  276.1 18.4 %copy-start.13 = (bf16[1024,128]{1,0:T(8,128)(2,1)S(1)}, bf16[1024,128]{1,0:T(8,128)(2,1)}, u32[]{:S(2)}) copy-start(bf16[1024,128]{1,0:T(8,128)(2,1)} %copy-done.12) | copy-start | bytes 786436
  276.1 18.4 %copy-start.16 = (bf16[1024,128]{1,0:T(8,128)(2,1)S(1)}, bf16[1024,128]{1,0:T(8,128)(2,1)}, u32[]{:S(2)}) copy-start(bf16[1024,128]{1,0:T(8,128)(2,1)} %copy-done.14) | copy-start | bytes 786436
  286.9 7.6 %copy-start.11 = (bf16[1,64,4096]{2,1,0:T(8,128)(2,1)}, bf16[1,64,4096]{2,1,0:T(8,128)(2,1)S(1)}, u32[]{:S(2)}) copy-start(bf16[1,64,4096]{2,1,0:T(8,128)(2,1)S(1)} %collective-permute-done.6) | copy-start | bytes 1572868
  286.9 16.6 %slice-start.2 = ((s8[8388608]{0:T(1024)(128)(4,1)}), s8[4194304]{0:T(1024)(128)(4,1)S(1)}, s32[]{:S(2)}) async-start(s8[8388608]{0:T(1024)(128)(4,1)} %bitcast.171), calls=%async_computation.9 | async-start | bytes 8388608
  294.5 9.0 %slice-start.3 = ((s8[8388608]{0:T(1024)(128)(4,1)}), s8[4194304]{0:T(1024)(128)(4,1)S(1)}, s32[]{:S(2)}) async-start(s8[8388608]{0:T(1024)(128)(4,1)} %bitcast.171), calls=%async_computation.10 | async-start | bytes 8388608
  303.5 123.1 %copy-start.17 = (f32[1,4096]{1,0:T(1,128)S(1)}, f32[1,4096]{1,0:T(1,128)}, u32[]{:S(2)}) copy-start(f32[1,4096]{1,0:T(1,128)} %param.12) | copy-start | bytes 49156
  303.6 124.6 %copy-start.4 = (bf16[1,64,4096]{2,1,0:T(8,128)(2,1)S(1)}, bf16[1,64,4096]{2,1,0:T(8,128)(2,1)}, u32[]{:S(2)}) copy-start(bf16[1,64,4096]{2,1,0:T(8,128)(2,1)} %param.11) | copy-start | bytes 1572868
  326.0 163.9 %collective-permute-start.1 = (bf16[1,64,4096]{2,1,0:T(8,128)(2,1)}, bf16[1,64,4096]{2,1,0:T(8,128)(2,1)}, u32[]{:S(2)}, u32[]{:S(2)}) collective-permute-start(bf16[1,64,4096]{2,1,0:T(8,128)(2,1)} %fusion.58), channel_id=1, source_target_pairs={{0,16},{16,32},{32,48},{48,64},{64,80},{80,96},{96,112},{112,0},{1... | collective-permute-start | bytes 1572872 | tf_op jit(solution)/shard_map/ppermute | solution.py:24
  428.2 66.3 %copy-start.1 = (bf16[1,256,4096]{2,1,0:T(8,128)(2,1)S(1)}, bf16[1,256,4096]{2,1,0:T(8,128)(2,1)}, u32[]{:S(2)}) copy-start(bf16[1,256,4096]{2,1,0:T(8,128)(2,1)} %param.15) | copy-start | bytes 6291460
  430.6 59.3 %collective-permute-start.5 = (bf16[1,64,4096]{2,1,0:T(8,128)(2,1)}, bf16[1,64,4096]{2,1,0:T(8,128)(2,1)S(1)}, u32[]{:S(2)}, u32[]{:S(2)}) collective-permute-start(bf16[1,64,4096]{2,1,0:T(8,128)(2,1)} %fusion.59), channel_id=1, source_target_pairs={{0,112},{16,0},{32,16},{48,32},{64,48},{80,64},{96,80},{112,96},{1... | collective-permute-start | bytes 1572872 | tf_op jit(solution)/shard_map/ppermute | solution.py:24
Sparse Core Ops, SparseCore 0:
  10.3 55.7 all-gather.5
  68.3 52.9 all-gather.3
  123.6 52.9 all-gather.7
  226.7 97.3 reduce-scatter.2
  326.3 100.2 reduce-scatter.4
where the time goes:
time: 510 us; the launch traced here: 501 us
  waiting for transfers between devices  270 us (53%)
  matrix products  124 us (24%)
  blocking collectives  49.2 us (10%)
  other arithmetic  22.1 us (4%)
  between operations  15.1 us (3%)
  starting transfers between devices  13.6 us (3%)
  local copies, waits for them, and re-layouts  6.93 us (1%)
    reduce_scatter x1, waiting for transfers between devices, body(): lax.psum_scatter((first + jnp.einsum('ta,ca->tc', d_keyval, weight_keyval...  98.8 us
    all_gather x1, waiting for transfers between devices, body(): combined = project(lax.all_gather(normed, 'dp', axis=0, tiled=True))  49.5 us
    unnamed x1, blocking collectives  49.2 us
    all_gather x1, waiting for transfers between devices, body(): normed_all = lax.all_gather(normed, 'dp', axis=0, tiled=True)  48.4 us
    dot_general x4, matrix products, attend(): jnp.einsum('hqk,kd->qhd', weights, values, precision=lax.Precision.HIGHEST)  36.5 us
    all_gather x1, waiting for transfers between devices, body(): upstream_all = lax.all_gather(upstream, 'dp', axis=0, tiled=True)  34.8 us
    ppermute x4, waiting for transfers between devices, passed_along(): return lax.ppermute(value, axis, pairs)  21.4 us
    dot_general x4, matrix products, attend(): jnp.einsum('qhd,kd->hqk', queries, key_rows, precision=lax.Precision.HIGH...  16.9 us
  transfers between devices with their start and end apart: 12, of which 7 were waited for; matrix products, arithmetic and copies ran while one was open for 22% of the time, Pallas kernels for 0%

commit v1 on v0

v1 whole, which is shorter than its diff:
```python
import functools
import math

import jax
import jax.numpy as jnp
from jax import lax
from jax.experimental import pallas as pl
from jax.experimental.pallas import tpu as pltpu
from jax.sharding import PartitionSpec as P

LANGS = 16
EPSILON = 1e-05
NEG_FILL = -1e30
MESH = pl.DeviceIdType.MESH
BF16 = jnp.bfloat16
F32 = jnp.float32

SHARD = 64
A, A0, A1 = (0, 32), (0, 16), (16, 16)
B, B0, B1 = (32, 32), (32, 16), (48, 16)
WHOLE = (0, 64)
PLACES = [(0, 0), (0, 1), (-1, 0), (1, 0), (2, 0), (-1, 1), (1, 1), (2, 1)]


def dot(a, b, dims=((1,), (0,))):
    return lax.dot_general(a, b, (dims, ((), ())), preferred_element_type=F32)


class Place:
    def __init__(self):
        self.s = lax.axis_index("section")
        self.d = lax.axis_index("dp")
        self.x = self.d // 4
        self.y = lax.rem(self.d // 2, 2)
        self.c = lax.rem(self.d, 2)

    def index(self, dx, dy, flip=0):
        x = lax.rem(self.x + dx + 4, 4)
        y = self.y if dy == 0 else 1 - self.y
        c = self.c if flip == 0 else 1 - self.c
        return x * 4 + y * 2 + c

    def row(self, dx, dy, part, flip=0):
        start = self.index(dx, dy, flip) * SHARD + part[0]
        return pl.ds(pl.multiple_of(start, 16), part[1])

    def peer(self, dx, dy, flip=0):
        return (self.s, self.index(dx, dy, flip))

    def relay(self, steps):
        return (lax.rem(self.s + steps + 8, 8), self.d)


class Mover:
    def __init__(self, send_sem, recv_sem):
        self.send_sem, self.recv_sem = send_sem, recv_sem
        self.open = []

    def send(self, key, src, dst, target):
        copy = pltpu.make_async_remote_copy(
            src_ref=src, dst_ref=dst, send_sem=self.send_sem.at[key], recv_sem=self.recv_sem.at[key],
            device_id=target, device_id_type=MESH,
        )
        copy.start()
        self.open.append(copy)

    def take(self, key, dst, source):
        pltpu.make_async_remote_copy(
            src_ref=dst, dst_ref=dst, send_sem=self.send_sem.at[key], recv_sem=self.recv_sem.at[key],
            device_id=source, device_id_type=MESH,
        ).wait_recv()

    def drain(self):
        for copy in self.open:
            copy.wait_send()
        self.open = []


class Gather:
    def __init__(self, place, buf, send_sem, recv_sem):
        self.at, self.buf = place, buf
        self.move = Mover(send_sem, recv_sem)

    def go(self, key, where, part, to):
        rows = self.buf.at[self.at.row(*where, part)]
        self.move.send(key, rows, rows, self.at.peer(*to))

    def sib(self, where, part):
        key = 18 + 2 * PLACES.index(where) + (0 if part == A else 1)
        rows = self.buf.at[self.at.row(*where, part)]
        self.move.send(key, rows, rows, self.at.peer(0, 0, 1))

    def got(self, key, where, part):
        self.move.take(key, self.buf.at[self.at.row(*where, part)], self.at.peer(0, 1))

    def start(self):
        own, right, left, up = (0, 0), (1, 0), (-1, 0), (0, 1)
        self.go(13, own, B, up)
        self.go(0, own, A, right)
        self.go(6, own, A, left)
        self.go(12, own, A, up)
        self.go(1, own, B, right)
        self.go(7, own, B, left)
        self.sib(own, A)
        self.sib(own, B)

    def mid(self):
        right, left, up = (1, 0), (-1, 0), (0, 1)
        self.got(13, up, B)
        self.go(2, up, B, right)
        self.go(8, up, B, left)
        self.got(0, left, A)
        self.go(3, left, A0, right)
        self.go(14, left, A, up)
        self.got(6, right, A)
        self.go(9, right, A1, left)
        self.go(15, right, A, up)
        self.sib(up, B)
        self.sib(left, A)
        self.sib(right, A)
        self.got(1, left, B)
        self.go(4, left, B0, right)
        self.got(7, right, B)
        self.go(10, right, B1, left)
        self.sib(left, B)
        self.sib(right, B)

    def mid2(self):
        right, left, up = (1, 0), (-1, 0), (0, 1)
        self.got(2, (-1, 1), B)
        self.go(5, (-1, 1), B0, right)
        self.got(8, (1, 1), B)
        self.go(11, (1, 1), B1, left)
        self.sib((-1, 1), B)
        self.sib((1, 1), B)
        self.got(3, (2, 0), A0)
        self.got(9, (2, 0), A1)
        self.go(16, (2, 0), A, up)
        self.sib((2, 0), A)

    def fin(self):
        self.got(12, (0, 1), A)
        self.sib((0, 1), A)
        self.got(14, (-1, 1), A)
        self.sib((-1, 1), A)
        self.got(15, (1, 1), A)
        self.sib((1, 1), A)
        self.got(4, (2, 0), B0)
        self.got(10, (2, 0), B1)
        self.sib((2, 0), B)
        self.got(5, (2, 1), B0)
        self.got(11, (2, 1), B1)
        self.sib((2, 1), B)
        self.got(16, (2, 1), A)
        self.sib((2, 1), A)
        for i, where in enumerate(PLACES):
            for j, part in enumerate((A, B)):
                self.move.take(18 + 2 * i + j, self.buf.at[self.at.row(*where, part, 1)], self.at.peer(0, 0, 1))


SIZES = [16, 16, 16, 32, 32, 32, 16, 16, 16, 32, 32, 32, 32, 32, 32, 32, 32] + [64] * 8
OFFSETS = [sum(SIZES[:i]) for i in range(len(SIZES))]


class Scatter:
    ORDER = [2, 1, -1, 0]

    def __init__(self, place, buf, land, send_sem, recv_sem):
        self.at, self.buf, self.land = place, buf, land
        self.move = Mover(send_sem, recv_sem)

    def slot(self, key):
        return self.land.at[pl.ds(OFFSETS[key], SIZES[key])]

    def go(self, key, where, part, to):
        self.move.send(key, self.buf.at[self.at.row(*where, part)], self.slot(key), self.at.peer(*to))

    def add(self, key, where, part):
        self.move.take(key, self.slot(key), self.at.peer(0, 1))
        rows = self.at.row(*where, part)
        total = self.buf[rows, :].astype(F32) + self.slot(key)[...].astype(F32)
        self.buf[rows, :] = total.astype(BF16)

    def block(self, dx):
        return pl.multiple_of(lax.rem(self.at.x + dx + 4, 4) * 256, 256)

    def share(self, dx):
        for dy in (1, 0):
            key = 17 + 2 * self.ORDER.index(dx) + dy
            rows = self.buf.at[self.at.row(dx, dy, WHOLE, 1)]
            self.move.send(key, rows, self.slot(key), self.at.peer(0, 0, 1))

    def join(self, dx):
        right, left, up = (1, 0), (-1, 0), (0, 1)
        for dy in (1, 0):
            self.add(17 + 2 * self.ORDER.index(dx) + dy, (dx, dy), WHOLE)
        if dx == 2:
            self.go(0, (2, 1), B0, left)
            self.go(6, (2, 1), B1, right)
            self.go(12, (2, 1), A, up)
            self.go(1, (2, 0), B0, left)
            self.go(7, (2, 0), B1, right)
        else:
            self.go({-1: 13, 1: 14, 0: 15}[dx], (dx, 1), A, up)

    def cross(self):
        right, left = (1, 0), (-1, 0)
        self.add(12, (2, 0), A)
        self.go(2, (2, 0), A0, left)
        self.go(8, (2, 0), A1, right)
        self.add(0, (-1, 1), B0)
        self.go(3, (-1, 1), B, left)
        self.add(6, (1, 1), B1)
        self.go(9, (1, 1), B, right)
        self.add(1, (-1, 0), B0)
        self.go(4, (-1, 0), B, left)
        self.add(7, (1, 0), B1)
        self.go(10, (1, 0), B, right)

    def cross2(self):
        right, left, up = (1, 0), (-1, 0), (0, 1)
        self.add(13, (-1, 0), A)
        self.add(2, (-1, 0), A0)
        self.go(5, (-1, 0), A, left)
        self.add(14, (1, 0), A)
        self.add(8, (1, 0), A1)
        self.go(11, (1, 0), A, right)
        self.add(3, (0, 1), B)
        self.add(9, (0, 1), B)
        self.go(16, (0, 1), B, up)

    def total(self, part):
        keys = (15, 5, 11) if part == A else (4, 10, 16)
        out = self.buf[self.at.row(0, 0, part), :].astype(F32)
        for key in keys:
            self.move.take(key, self.slot(key), self.at.peer(0, 1))
            out = out + self.slot(key)[...].astype(F32)
        return out


def softmax_block(q_blk, keys, first):
    rows, length = q_blk.shape[0], keys.shape[0]
    scale = 1.0 / math.sqrt(q_blk.shape[1])
    scores = dot(q_blk, keys, ((1,), (1,)))
    row_index = lax.broadcasted_iota(jnp.int32, (rows, length), 0) + first
    col_index = lax.broadcasted_iota(jnp.int32, (rows, length), 1)
    scores = jnp.where(col_index <= row_index, scores, NEG_FILL)
    weights = jnp.exp((scores - jnp.max(scores, axis=-1, keepdims=True)) * scale)
    return weights, jnp.sum(weights, axis=-1, keepdims=True)


def kernel(
    inc, parked, cot, gain, tw, wq_hbm, wkv_hbm, wo_hbm,
    next_out, back_out, parkn_out, qg_out, kg_out, og_out, dgain_out,
    g, land, wq, wkv, wo, stash, fwd_rows, back_rows, q, kv, att, d_out, dq, dk, dv, dkv_send, dkv_recv, dkv,
    ag_send, ag_recv, rs_send, rs_recv, misc_send, misc_recv, local_sem,
):
    at = Place()
    length = g.shape[1]
    blocks = length // 256

    barrier = pltpu.get_barrier_semaphore()
    peers = [at.peer(1, 0), at.peer(-1, 0), at.peer(0, 1), at.peer(0, 0, 1), at.relay(4), at.relay(1), at.relay(-1)]
    for peer in peers:
        pl.semaphore_signal(barrier, inc=1, device_id=peer, device_id_type=MESH)
    loads = [
        pltpu.make_async_copy(src, dst, local_sem.at[i])
        for i, (src, dst) in enumerate(((wq_hbm, wq), (wkv_hbm, wkv), (wo_hbm, wo)))
    ]
    for load in loads:
        load.start()

    own = at.row(0, 0, WHOLE)

    def inverse_rms(values):
        return lax.rsqrt(jnp.mean(values * values, axis=-1, keepdims=True) + EPSILON)

    values = inc[...].astype(F32)
    g[0, own, :] = (values * inverse_rms(values) * gain[...]).astype(BF16)
    g[1, own, :] = (cot[...].astype(F32) * tw[...]).astype(BF16)

    pl.semaphore_wait(barrier, len(peers))
    misc = Mover(misc_send, misc_recv)
    misc.send(0, parked, stash, at.relay(4))
    ag = [Gather(at, g.at[i], ag_send.at[i], ag_recv.at[i]) for i in range(3)]
    ag[0].start()
    ag[1].start()
    misc.send(1, inc, parkn_out, at.relay(4))
    ag[0].mid()

    misc.take(0, stash, at.relay(4))
    values = stash[...].astype(F32)
    g[2, own, :] = (values * inverse_rms(values) * gain[...]).astype(BF16)
    ag[2].start()
    ag[0].mid2()
    ag[1].mid()
    ag[0].fin()
    loads[0].wait()
    loads[1].wait()
    core = at.c

    def project(source, slot):
        def step(i, carry):
            rows = pl.ds(pl.multiple_of(i * 256, 256), 256)
            piece = g[source, rows, :]
            q[slot, rows, :] = dot(piece, wq[...]).astype(BF16)
            kv[slot, core, rows, :] = dot(piece, wkv[...]).astype(BF16)
            return carry

        lax.fori_loop(0, blocks, step, 0)
        misc.send(2 + slot, kv.at[slot, core], kv.at[slot, core], at.peer(0, 0, 1))

    def keyval_arrived(slot):
        misc.take(2 + slot, kv.at[slot, 1 - core], at.peer(0, 0, 1))

    project(0, 0)
    ag[1].mid2()
    ag[2].mid()
    keyval_arrived(0)

    def attend(head, carry):
        cols = pl.ds(pl.multiple_of(head * 128, 128), 128)
        for i in range(blocks):
            rows, seen = pl.ds(i * 256, 256), pl.ds(0, (i + 1) * 256)
            weights, norm = softmax_block(q[0, rows, cols], kv[0, 0, seen, :], i * 256)
            att[0, rows, cols] = (dot(weights.astype(BF16), kv[0, 1, seen, :]) / norm).astype(BF16)
        return carry

    lax.fori_loop(0, 2, attend, 0)
    ag[1].fin()
    ag[2].mid2()
    loads[2].wait()
    ag[0].move.drain()

    rs = [Scatter(at, g.at[i], land.at[i], rs_send.at[i], rs_recv.at[i]) for i in range(2)]

    def produce_forward(dx):
        rows = pl.ds(rs[0].block(dx), 256)
        piece = att[0, rows, :]

        def step(j, carry):
            cols = pl.ds(pl.multiple_of(j * 512, 512), 512)
            g[0, rows, cols] = dot(piece, wo[:, cols]).astype(BF16)
            return carry

        lax.fori_loop(0, g.shape[2] // 512, step, 0)
        rs[0].share(dx)

    for dx in Scatter.ORDER:
        produce_forward(dx)

    def cotangent_step(i, carry):
        rows = pl.ds(pl.multiple_of(i * 256, 256), 256)
        d_out[rows, :] = dot(g[1, rows, :], wo[...], ((1,), (1,))).astype(BF16)
        return carry

    lax.fori_loop(0, blocks, cotangent_step, 0)
    ag[2].fin()
    for dx in Scatter.ORDER:
        rs[0].join(dx)
    project(2, 1)
    keyval_arrived(1)
    rs[0].cross()

    dk[...] = jnp.zeros_like(dk)
    dv[...] = jnp.zeros_like(dv)
    scale = 1.0 / math.sqrt(dk.shape[1])

    def attend_back(head):
        cols = pl.ds(head * 128, 128)
        for i in range(blocks):
            rows, seen = pl.ds(i * 256, 256), pl.ds(0, (i + 1) * 256)
            q_blk, keys, vals = q[1, rows, cols], kv[1, 0, seen, :], kv[1, 1, seen, :]
            weights, norm = softmax_block(q_blk, keys, i * 256)
            weights = weights / norm
            rounded = weights.astype(BF16)
            att[1, rows, cols] = dot(rounded, vals).astype(BF16)
            d_blk = d_out[rows, cols]
            d_weights = dot(d_blk, vals, ((1,), (1,)))
            delta = jnp.sum(weights * d_weights, axis=-1, keepdims=True)
            d_scores = (weights * (d_weights - delta) * scale).astype(BF16)
            dq[rows, cols] = dot(d_scores, keys).astype(BF16)
            dk[seen, :] += dot(d_scores, q_blk, ((0,), (0,)))
            dv[seen, :] += dot(rounded, d_blk, ((0,), (0,)))

    attend_back(0)
    rs[0].cross2()
    attend_back(1)
    even = core == 0
    dkv_send[...] = jnp.where(even, dv[...], dk[...]).astype(BF16)
    misc.send(4, dkv_send, dkv_recv, at.peer(0, 0, 1))

    att_t = att[1].T

    def output_grad_step(j, carry):
        cols = pl.ds(pl.multiple_of(j * 512, 512), 512)
        wo[:, cols] = dot(att_t, g[1, :, cols]).astype(BF16)
        return carry

    lax.fori_loop(0, g.shape[2] // 512, output_grad_step, 0)
    og_copy = pltpu.make_async_copy(wo, og_out, local_sem.at[3])
    og_copy.start()

    misc.take(4, dkv_recv, at.peer(0, 0, 1))
    dkv[...] = (jnp.where(even, dk[...], dv[...]) + dkv_recv[...].astype(F32)).astype(BF16)
    ag[1].move.drain()

    def produce_back(dx):
        rows = pl.ds(rs[1].block(dx), 256)
        dq_blk, dkv_blk = dq[rows, :], dkv[rows, :]

        def step(j, carry):
            cols = pl.ds(pl.multiple_of(j * 512, 512), 512)
            term = dot(dq_blk, wq[cols, :], ((1,), (1,))) + dot(dkv_blk, wkv[cols, :], ((1,), (1,)))
            g[1, rows, cols] = term.astype(BF16)
            return carry

        lax.fori_loop(0, g.shape[2] // 512, step, 0)
        rs[1].share(dx)

    produce_back(2)
    produce_back(1)
    rs[1].join(2)
    produce_back(-1)
    rs[1].join(1)
    produce_back(0)
    rs[1].join(-1)
    rs[1].join(0)

    for part in (A, B):
        rows = pl.ds(*part)
        fwd_rows[rows, :] = (inc[rows, :].astype(F32) + rs[0].total(part)).astype(BF16)
    misc.send(5, fwd_rows, next_out, at.relay(1))
    rs[1].cross()

    grad_t = jnp.concatenate([dq[...], dkv[...]], axis=1).T

    def weight_grad_step(j, carry):
        cols = pl.ds(pl.multiple_of(j * 512, 512), 512)
        piece = dot(grad_t, g[2, :, cols]).astype(BF16).T
        wq[cols, :] = piece[:, :256]
        wkv[cols, :] = piece[:, 256:]
        return carry

    half = g.shape[2] // 1024
    lax.fori_loop(0, half, weight_grad_step, 0)
    rs[1].cross2()
    lax.fori_loop(half, 2 * half, weight_grad_step, 0)
    qg_copy = pltpu.make_async_copy(wq, qg_out, local_sem.at[4])
    kg_copy = pltpu.make_async_copy(wkv, kg_out, local_sem.at[5])
    qg_copy.start()
    kg_copy.start()

    d_gain = jnp.zeros((1, g.shape[2]), F32)
    for part in (A, B):
        rows = pl.ds(*part)
        d_normed = rs[1].total(part)
        values = stash[rows, :].astype(F32)
        inverse = inverse_rms(values)
        d_gain = d_gain + jnp.sum(d_normed * (values * inverse), axis=0, keepdims=True)
        scaled = d_normed * gain[...]
        inner = jnp.mean(scaled * values, axis=-1, keepdims=True)
        d_rows = inverse * scaled - values * (inverse * inverse * inverse * inner)
        upstream = (cot[rows, :].astype(F32) * tw[rows, :]).astype(BF16).astype(F32)
        back_rows[rows, :] = (upstream + d_rows).astype(BF16)
    misc.send(6, back_rows, back_out, at.relay(-1))
    dgain_out[...] = d_gain

    for copy in (og_copy, qg_copy, kg_copy):
        copy.wait()
    for mover in (ag[2].move, rs[0].move, rs[1].move):
        mover.drain()
    misc.take(1, parkn_out, at.relay(4))
    misc.take(5, next_out, at.relay(-1))
    misc.take(6, back_out, at.relay(1))
    misc.drain()


def cycle(inc, parked, cot, gain, tw, wq, wkv, wo):
    tokens, width = inc.shape
    length = tokens * lax.axis_size("dp")
    any_spec = pl.BlockSpec(memory_space=pl.ANY)
    vmem_spec = pl.BlockSpec(memory_space=pltpu.VMEM)
    block = jax.ShapeDtypeStruct((tokens, width), BF16)
    shapes = [block, block, block] + [jax.ShapeDtypeStruct(w.shape, BF16) for w in (wq, wkv, wo)]
    shapes.append(jax.ShapeDtypeStruct((1, width), F32))
    heads_width, head_dim = wq.shape[1], wkv.shape[1]
    scratch = [
        pltpu.VMEM((3, length, width), BF16),
        pltpu.VMEM((2, sum(SIZES), width), BF16),
        pltpu.VMEM(wq.shape, BF16),
        pltpu.VMEM(wkv.shape, BF16),
        pltpu.VMEM(wo.shape, BF16),
        pltpu.VMEM((tokens, width), BF16),
        pltpu.VMEM((tokens, width), BF16),
        pltpu.VMEM((tokens, width), BF16),
        pltpu.VMEM((2, length, heads_width), BF16),
        pltpu.VMEM((2, 2, length, head_dim), BF16),
        pltpu.VMEM((2, length, heads_width), BF16),
        pltpu.VMEM((length, heads_width), BF16),
        pltpu.VMEM((length, heads_width), BF16),
        pltpu.VMEM((length, head_dim), F32),
        pltpu.VMEM((length, head_dim), F32),
        pltpu.VMEM((length, head_dim), BF16),
        pltpu.VMEM((length, head_dim), BF16),
        pltpu.VMEM((length, head_dim), BF16),
        pltpu.SemaphoreType.DMA((3, 34)),
        pltpu.SemaphoreType.DMA((3, 34)),
        pltpu.SemaphoreType.DMA((2, 25)),
        pltpu.SemaphoreType.DMA((2, 25)),
        pltpu.SemaphoreType.DMA((7,)),
        pltpu.SemaphoreType.DMA((7,)),
        pltpu.SemaphoreType.DMA((6,)),
    ]
    return pl.pallas_call(
        kernel,
        out_shape=shapes,
        in_specs=[vmem_spec, any_spec, vmem_spec, vmem_spec, vmem_spec, any_spec, any_spec, any_spec],
        out_specs=[any_spec] * 6 + [vmem_spec],
        scratch_shapes=scratch,
        compiler_params=pltpu.CompilerParams(
            collective_id=0, has_side_effects=True, vmem_limit_bytes=60 * 2**20
        ),
        cost_estimate=pl.CostEstimate(flops=24 * 10**9, bytes_accessed=2 * 10**7, transcendentals=4 * 10**6),
        name="relay_cycle",
    )(inc, parked, cot, gain, tw, wq, wkv, wo)


def body(
    incoming,
    parked,
    cotangent,
    norm_gain,
    query_weight,
    keyval_weight,
    output_weight,
    teacher_id,
    language_id,
):
    sections = lax.axis_size("section")
    section_rank = lax.axis_index("section")
    token_weight = jnp.power(0.5, teacher_id.astype(F32)) * (0.5 + language_id.astype(F32) / (LANGS - 1))
    token_weight = jnp.where(section_rank == sections - 1, token_weight, 1.0)[:, None]
    next_input, input_grad, parked_next, query_grad, keyval_grad, output_grad, d_gain = cycle(
        incoming[0], parked[0], cotangent[0], norm_gain, token_weight,
        query_weight[0], keyval_weight[0], output_weight[0],
    )
    ranks = lax.axis_size("dp")
    parts = lax.all_to_all(d_gain.reshape(ranks, -1), "dp", 0, 0)
    gain_grad = jnp.sum(parts, axis=0)
    return tuple(
        item[None]
        for item in (next_input, input_grad, parked_next, query_grad, keyval_grad, output_grad, gain_grad)
    )


def solution(mesh):
    return jax.shard_map(
        body,
        mesh=mesh,
        in_specs=(
            P("section", "dp", None),
            P("section", "dp", None),
            P("section", "dp", None),
            P("section", None),
            P("section", None, "dp"),
            P("section", None, "dp"),
            P("section", "dp", None),
            P("dp"),
            P("dp"),
        ),
        out_specs=(
            P("section", "dp", None),
            P("section", "dp", None),
            P("section", "dp", None),
            P("section", None, "dp"),
            P("section", None, "dp"),
            P("section", "dp", None),
            P("section", "dp"),
        ),
        check_vma=False,
    )
```

time: 510 us -> 212 us (0.42); the launches traced: 501 us -> 211 us
  waiting for transfers between devices: 270 us -> 5.85 us
  Pallas kernels: 0 us -> 187 us
  matrix products: 124 us -> 0 us
  blocking collectives: 49.2 us -> 0 us
  other arithmetic: 22.1 us -> 1.28 us
  between operations: 15.1 us -> 0.66 us
  starting transfers between devices: 13.6 us -> 4.89 us
    pallas_call x0 -> x1, Pallas kernels: none -> 187 us  [cycle(): pl.pallas_call(kernel, out_shape=shapes, in_specs=[vmem_spec, any_spec, v...]
    all_gather x3 -> x0, waiting for transfers between devices: 133 us -> none  [the longest x1 49.5 us: body(): combined = project(lax.all_gather(normed, 'dp', axis=0, tiled=True))]
    dot_general x19 -> x0, matrix products: 124 us -> none  [the longest x4 36.5 us: attend(): jnp.einsum('hqk,kd->qhd', weights, values, precision=lax.Precision.HIGHEST)]
    reduce_scatter x2 -> x0, waiting for transfers between devices: 116 us -> none  [the longest x1 98.8 us: body(): lax.psum_scatter((first + jnp.einsum('ta,ca->tc', d_keyval, weight_keyval...]
    unnamed x1 -> x0, blocking collectives: 49.2 us -> none
    ppermute x7 -> x0, waiting for transfers between devices: 21.4 us -> none  [the longest x4 21.4 us: passed_along(): return lax.ppermute(value, axis, pairs)]
    ppermute x7 -> x0, starting transfers between devices: 13.4 us -> none  [the longest x4 12.3 us: passed_along(): return lax.ppermute(value, axis, pairs)]
    mul x2 -> x0, other arithmetic: 8.58 us -> none  [the longest x1 7.77 us: attend(): jnp.einsum('qhd,kd->hqk', queries, key_rows, precision=lax.Precision.HIGH...]
  transfers between devices with their start and end apart: 12 -> 1, of which waited for: 7 -> 1; matrix products, arithmetic and copies ran while one was open for 22% -> 0% of each run, Pallas kernels for 0% -> 0%
where the time goes in v1:
time: 212 us; the launch traced here: 211 us
  Pallas kernels  187 us (88%)
  local copies, waits for them, and re-layouts  11.6 us (5%)
  waiting for transfers between devices  5.85 us (3%)
  starting transfers between devices  4.89 us (2%)
    pallas_call x1, Pallas kernels, cycle(): pl.pallas_call(kernel, out_shape=shapes, in_specs=[vmem_spec, any_spec, v...  187 us
    unnamed x12, local copies, waits for them, and re-layouts  10.9 us
    all_to_all x1, waiting for transfers between devices, body(): parts = lax.all_to_all(d_gain.reshape(ranks, -1), 'dp', 0, 0)  5.85 us
    all_to_all x1, starting transfers between devices, body(): parts = lax.all_to_all(d_gain.reshape(ranks, -1), 'dp', 0, 0)  4.89 us
  transfers between devices with their start and end apart: 1, of which 1 were waited for; matrix products, arithmetic and copies ran while one was open for 0% of the time, Pallas kernels for 0%

profile of v1, /device:TPU:1, one launch (start us, length us, event | category | flops | bytes accessed | tf_op | source)
XLA Modules:
  0.0 211.2 jit_solution(821968507371827756)
XLA Ops:
  0.6 0.7 fusion
  1.3 0.7 copy.17.tw
  2.0 187.0 %relay_cycle.1 = (bf16[64,4096]{1,0:T(8,128)(2,1)}, bf16[64,4096]{1,0:T(8,128)(2,1)}, bf16[64,4096]{1,0:T(8,128)(2,1)}, bf16[4096,256]{1,0:T(8,128)(2,1)}, bf16[...) custom-call(bf16[64,4096]{1,0:T(8,128)(2,1)} %bitcast.27, bf16[64,4096]{1,0:T(8,128)(2,1)} %bitcast.28, ...), custom_call_target="tpu_custom_call" | custom-call | flops 24000000000 | bytes 20000000 | tf_op jit(solution)/shard_map/relay_cycle/pallas_call | solution.py:515
  189.0 0.0 copy-start.1
  189.0 4.9 %all-to-all-start = ((f32[16,1,256]{2,1,0:T(1,128)}), f32[16,1,256]{2,1,0:T(1,128)S(1)}, u32[]{:S(2)}, u32[]{:S(2)}) async-start(f32[16,1,256]{2,1,0:T(1,128)} %bitcast.22), calls=%async_computation | async-start | bytes 32768 | tf_op jit(solution)/shard_map/all_to_all | solution.py:549
  193.9 5.9 %all-to-all-done = f32[16,1,256]{2,1,0:T(1,128)S(1)} async-done(((f32[16,1,256]{2,1,0:T(1,128)}), f32[16,1,256]{2,1,0:T(1,128)S(1)}, u32[]{:S(2)}, u32[]{:S(2)}) %all-to-all-start) | async-done | bytes 16416 | tf_op jit(solution)/shard_map/all_to_all | solution.py:549
  199.8 0.6 reduce_sum.9
  200.4 1.9 copy.25
  202.2 1.9 copy.26
  204.1 1.9 copy.27
  206.0 0.0 copy-done.1
  206.0 0.0 copy-start.2
  206.0 1.3 copy.28
  207.3 0.6 copy-done.2
  207.9 0.0 copy-start
  207.9 1.0 copy.29
  208.9 1.0 copy-done
  209.9 1.3 copy.30
Async XLA Ops:
  189.0 17.0 %copy-start.1 = (bf16[4096,256]{1,0:T(8,128)(2,1)S(1)}, bf16[4096,256]{1,0:T(8,128)(2,1)}, u32[]{:S(2)}) copy-start(bf16[4096,256]{1,0:T(8,128)(2,1)} %get-tuple-element.17) | copy-start | bytes 6291460
  189.0 10.7 %all-to-all-start = ((f32[16,1,256]{2,1,0:T(1,128)}), f32[16,1,256]{2,1,0:T(1,128)S(1)}, u32[]{:S(2)}, u32[]{:S(2)}) async-start(f32[16,1,256]{2,1,0:T(1,128)} %bitcast.22), calls=%async_computation | async-start | bytes 32768 | tf_op jit(solution)/shard_map/all_to_all | solution.py:549
  206.0 2.0 copy-start.2
  207.9 2.0 copy-start

commit v2 on v1

v2 whole, which is shorter than its diff:
```python
import functools
import math

import jax
import jax.numpy as jnp
from jax import lax
from jax.experimental import pallas as pl
from jax.experimental.pallas import tpu as pltpu
from jax.sharding import PartitionSpec as P

LANGS = 16
EPSILON = 1e-05
NEG_FILL = -1e30
MESH = pl.DeviceIdType.MESH
BF16 = jnp.bfloat16
F32 = jnp.float32

SHARD = 64
WHOLE = (0, 64)
PLACES = [(0, 0), (0, 1), (-1, 0), (1, 0), (2, 0), (-1, 1), (1, 1), (2, 1)]


def dot(a, b, dims=((1,), (0,))):
    return lax.dot_general(a, b, (dims, ((), ())), preferred_element_type=F32)


class Split:
    def __init__(self, low, a_cut, middle, b_cut, high):
        self.whole = (low, high - low)
        self.A, self.A0, self.A1 = (low, middle - low), (low, a_cut - low), (a_cut, middle - a_cut)
        self.B, self.B0, self.B1 = (middle, high - middle), (middle, b_cut - middle), (b_cut, high - b_cut)


EVEN = Split(0, 16, 32, 48, 64)
TILT_RIGHT = Split(0, 16, 16, 32, 64)
TILT_LEFT = Split(0, 0, 16, 48, 64)
UPPER = Split(0, 16, 16, 16, 32)
LOWER = Split(32, 32, 48, 64, 64)


class Place:
    def __init__(self):
        self.s = lax.axis_index("section")
        self.d = lax.axis_index("dp")
        self.x = self.d // 4
        self.y = lax.rem(self.d // 2, 2)
        self.c = lax.rem(self.d, 2)

    def index(self, dx, dy, flip=0):
        x = lax.rem(self.x + dx + 4, 4)
        y = self.y if dy == 0 else 1 - self.y
        c = self.c if flip == 0 else 1 - self.c
        return x * 4 + y * 2 + c

    def row(self, dx, dy, part, flip=0):
        start = self.index(dx, dy, flip) * SHARD + part[0]
        return pl.ds(pl.multiple_of(start, 16), part[1])

    def peer(self, dx, dy, flip=0):
        return (self.s, self.index(dx, dy, flip))

    def relay(self, steps):
        return (lax.rem(self.s + steps + 8, 8), self.d)


class Mover:
    def __init__(self, send_sem, recv_sem):
        self.send_sem, self.recv_sem = send_sem, recv_sem
        self.open = []

    def send(self, key, src, dst, target):
        copy = pltpu.make_async_remote_copy(
            src_ref=src, dst_ref=dst, send_sem=self.send_sem.at[key], recv_sem=self.recv_sem.at[key],
            device_id=target, device_id_type=MESH,
        )
        copy.start()
        self.open.append(copy)

    def take(self, key, dst, source):
        pltpu.make_async_remote_copy(
            src_ref=dst, dst_ref=dst, send_sem=self.send_sem.at[key], recv_sem=self.recv_sem.at[key],
            device_id=source, device_id_type=MESH,
        ).wait_recv()

    def drain(self):
        for copy in self.open:
            copy.wait_send()
        self.open = []


class Gather:
    def __init__(self, place, split, buf, send_sem, recv_sem):
        self.at, self.split, self.buf = place, split, buf
        self.move = Mover(send_sem, recv_sem)

    def go(self, key, where, part, to):
        if part[1]:
            rows = self.buf.at[self.at.row(*where, part)]
            self.move.send(key, rows, rows, self.at.peer(*to))

    def sib(self, where, part):
        key = 18 + 2 * PLACES.index(where) + (0 if part == self.split.A else 1)
        rows = self.buf.at[self.at.row(*where, part)]
        self.move.send(key, rows, rows, self.at.peer(0, 0, 1))

    def got(self, key, where, part):
        if part[1]:
            self.move.take(key, self.buf.at[self.at.row(*where, part)], self.at.peer(0, 1))

    def start(self):
        own, right, left, up = (0, 0), (1, 0), (-1, 0), (0, 1)
        self.go(13, own, self.split.B, up)
        self.go(0, own, self.split.A, right)
        self.go(6, own, self.split.A, left)
        self.go(12, own, self.split.A, up)
        self.go(1, own, self.split.B, right)
        self.go(7, own, self.split.B, left)
        self.sib(own, self.split.A)
        self.sib(own, self.split.B)

    def mid(self):
        right, left, up = (1, 0), (-1, 0), (0, 1)
        self.got(13, up, self.split.B)
        self.go(2, up, self.split.B, right)
        self.go(8, up, self.split.B, left)
        self.got(0, left, self.split.A)
        self.go(3, left, self.split.A0, right)
        self.go(14, left, self.split.A, up)
        self.got(6, right, self.split.A)
        self.go(9, right, self.split.A1, left)
        self.go(15, right, self.split.A, up)
        self.sib(up, self.split.B)
        self.sib(left, self.split.A)
        self.sib(right, self.split.A)
        self.got(1, left, self.split.B)
        self.go(4, left, self.split.B0, right)
        self.got(7, right, self.split.B)
        self.go(10, right, self.split.B1, left)
        self.sib(left, self.split.B)
        self.sib(right, self.split.B)

    def mid2(self):
        right, left, up = (1, 0), (-1, 0), (0, 1)
        self.got(2, (-1, 1), self.split.B)
        self.go(5, (-1, 1), self.split.B0, right)
        self.got(8, (1, 1), self.split.B)
        self.go(11, (1, 1), self.split.B1, left)
        self.sib((-1, 1), self.split.B)
        self.sib((1, 1), self.split.B)
        self.got(3, (2, 0), self.split.A0)
        self.got(9, (2, 0), self.split.A1)
        self.go(16, (2, 0), self.split.A, up)
        self.sib((2, 0), self.split.A)

    def fin(self):
        self.got(12, (0, 1), self.split.A)
        self.sib((0, 1), self.split.A)
        self.got(14, (-1, 1), self.split.A)
        self.sib((-1, 1), self.split.A)
        self.got(15, (1, 1), self.split.A)
        self.sib((1, 1), self.split.A)
        self.got(4, (2, 0), self.split.B0)
        self.got(10, (2, 0), self.split.B1)
        self.sib((2, 0), self.split.B)
        self.got(5, (2, 1), self.split.B0)
        self.got(11, (2, 1), self.split.B1)
        self.sib((2, 1), self.split.B)
        self.got(16, (2, 1), self.split.A)
        self.sib((2, 1), self.split.A)
        for i, where in enumerate(PLACES):
            for j, part in enumerate((self.split.A, self.split.B)):
                self.move.take(18 + 2 * i + j, self.buf.at[self.at.row(*where, part, 1)], self.at.peer(0, 0, 1))


class Scatter:
    ORDER = [2, 1, -1, 0]
    ROWS = 7 * SHARD + 8 * SHARD

    def __init__(self, place, split, buf, land, base, cols, send_sem, recv_sem):
        self.at, self.split, self.buf, self.land, self.cols = place, split, buf, land, cols
        self.move = Mover(send_sem, recv_sem)
        p = split
        parts = [p.B0, p.B0, p.A0, p.B, p.B, p.A, p.B1, p.B1, p.A1, p.B, p.B, p.A, p.A, p.A, p.A, p.A, p.B] + [p.whole] * 8
        self.sizes = [part[1] for part in parts]
        self.offsets = [base + sum(self.sizes[:i]) for i in range(len(parts))]

    def slot(self, key):
        return self.land.at[pl.ds(self.offsets[key], self.sizes[key]), self.cols]

    def go(self, key, where, part, to):
        if part[1]:
            rows = self.buf.at[self.at.row(*where, part), self.cols]
            self.move.send(key, rows, self.slot(key), self.at.peer(*to))

    def add(self, key, where, part):
        if part[1]:
            self.move.take(key, self.slot(key), self.at.peer(0, 1))
            rows = self.at.row(*where, part)
            total = self.buf[rows, self.cols].astype(F32) + self.slot(key)[...].astype(F32)
            self.buf[rows, self.cols] = total.astype(BF16)

    def block(self, dx):
        return pl.multiple_of(lax.rem(self.at.x + dx + 4, 4) * 256, 256)

    def share(self, dx):
        for dy in (1, 0):
            key = 17 + 2 * self.ORDER.index(dx) + dy
            rows = self.buf.at[self.at.row(dx, dy, self.split.whole, 1), self.cols]
            self.move.send(key, rows, self.slot(key), self.at.peer(0, 0, 1))

    def join(self, dx):
        right, left, up = (1, 0), (-1, 0), (0, 1)
        for dy in (1, 0):
            self.add(17 + 2 * self.ORDER.index(dx) + dy, (dx, dy), self.split.whole)
        if dx == 2:
            self.go(0, (2, 1), self.split.B0, left)
            self.go(6, (2, 1), self.split.B1, right)
            self.go(12, (2, 1), self.split.A, up)
            self.go(1, (2, 0), self.split.B0, left)
            self.go(7, (2, 0), self.split.B1, right)
        else:
            self.go({-1: 13, 1: 14, 0: 15}[dx], (dx, 1), self.split.A, up)

    def cross(self):
        right, left = (1, 0), (-1, 0)
        self.add(12, (2, 0), self.split.A)
        self.go(2, (2, 0), self.split.A0, left)
        self.go(8, (2, 0), self.split.A1, right)
        self.add(0, (-1, 1), self.split.B0)
        self.go(3, (-1, 1), self.split.B, left)
        self.add(6, (1, 1), self.split.B1)
        self.go(9, (1, 1), self.split.B, right)
        self.add(1, (-1, 0), self.split.B0)
        self.go(4, (-1, 0), self.split.B, left)
        self.add(7, (1, 0), self.split.B1)
        self.go(10, (1, 0), self.split.B, right)

    def cross2(self):
        right, left, up = (1, 0), (-1, 0), (0, 1)
        self.add(3, (0, 1), self.split.B)
        self.add(9, (0, 1), self.split.B)
        self.go(16, (0, 1), self.split.B, up)
        self.add(13, (-1, 0), self.split.A)
        self.add(2, (-1, 0), self.split.A0)
        self.go(5, (-1, 0), self.split.A, left)
        self.add(14, (1, 0), self.split.A)
        self.add(8, (1, 0), self.split.A1)
        self.go(11, (1, 0), self.split.A, right)

    def total(self, out, start=None):
        for part, keys in ((self.split.A, (15, 5, 11)), (self.split.B, (4, 10, 16))):
            rows = pl.ds(*part)
            whole = self.buf[self.at.row(0, 0, part), self.cols].astype(F32)
            for key in keys:
                self.move.take(key, self.slot(key), self.at.peer(0, 1))
                whole = whole + self.slot(key)[...].astype(F32)
            if start is not None:
                whole = whole + start[rows, self.cols].astype(F32)
            out[rows, self.cols] = whole.astype(out.dtype)


def softmax_block(q_blk, keys, first):
    rows, length = q_blk.shape[0], keys.shape[0]
    scale = 1.0 / math.sqrt(q_blk.shape[1])
    scores = dot(q_blk, keys, ((1,), (1,)))
    row_index = lax.broadcasted_iota(jnp.int32, (rows, length), 0) + first
    col_index = lax.broadcasted_iota(jnp.int32, (rows, length), 1)
    scores = jnp.where(col_index <= row_index, scores, NEG_FILL)
    weights = jnp.exp((scores - jnp.max(scores, axis=-1, keepdims=True)) * scale)
    return weights, jnp.sum(weights, axis=-1, keepdims=True)


def kernel(
    inc_hbm, parked, cot_hbm, gain, teacher, language, wq_hbm, wkv_hbm, wo_hbm,
    next_out, back_out, parkn_out, qg_out, kg_out, og_out, gain_out,
    g, land, wq, wkv, wo, og, inc, cot, stash, fwd_rows, back_rows, d_rows, q, kv, att, d_out, dq, dk, dv,
    dkv_send, dkv_recv, dkv, gain_send, gain_recv,
    ag_send, ag_recv, rs_send, rs_recv, misc_send, misc_recv, gs_send, gs_recv, local_sem,
):
    at = Place()
    length, width = g.shape[1], g.shape[2]
    blocks, ranks = length // 256, length // SHARD

    loads = [
        pltpu.make_async_copy(src, dst, local_sem.at[i])
        for i, (src, dst) in enumerate(
            ((inc_hbm, inc), (cot_hbm, cot), (wq_hbm, wq), (wkv_hbm, wkv), (wo_hbm, wo))
        )
    ]
    for load in loads:
        load.start()
    barrier = pltpu.get_barrier_semaphore()
    peers = [(at.s, lax.rem(at.d + k, ranks)) for k in range(1, ranks)] + [at.relay(4), at.relay(1), at.relay(-1)]
    for peer in peers:
        pl.semaphore_signal(barrier, inc=1, device_id=peer, device_id_type=MESH)

    own = at.row(0, 0, WHOLE)
    core = at.c

    def inverse_rms(values):
        return lax.rsqrt(jnp.mean(values * values, axis=-1, keepdims=True) + EPSILON)

    def normalized(rows):
        values = rows[...].astype(F32)
        return (values * inverse_rms(values) * gain[...]).astype(BF16)

    weight = jnp.exp2(-teacher[...].astype(F32)) * (0.5 + language[...].astype(F32) / (LANGS - 1))
    weight = jnp.where(at.s == lax.axis_size("section") - 1, weight, 1.0)
    square = lax.broadcasted_iota(jnp.int32, (SHARD, SHARD), 0) == lax.broadcasted_iota(jnp.int32, (SHARD, SHARD), 1)
    weight = jnp.sum(jnp.where(square, weight, 0.0), axis=1, keepdims=True)
    loads[0].wait()
    g[0, own, :] = normalized(inc)

    pl.semaphore_wait(barrier, len(peers))
    misc = Mover(misc_send, misc_recv)
    misc.send(0, parked, stash, at.relay(4))
    splits = (TILT_LEFT, EVEN, TILT_RIGHT)
    ag_f, ag_u, ag_b = [Gather(at, splits[i], g.at[i], ag_send.at[i], ag_recv.at[i]) for i in range(3)]
    ag_f.start()
    loads[1].wait()
    cot[...] = (cot[...].astype(F32) * weight).astype(BF16)
    g[1, own, :] = cot[...]
    ag_u.start()
    misc.send(1, inc, parkn_out, at.relay(4))
    ag_f.mid()
    misc.take(0, stash, at.relay(4))
    g[2, own, :] = normalized(stash)
    ag_b.start()
    ag_f.mid2()
    ag_u.mid()
    ag_f.fin()
    for load in loads[2:]:
        load.wait()

    def project(source, slot):
        def step(i, carry):
            rows = pl.ds(pl.multiple_of(i * 256, 256), 256)
            piece = g[source, rows, :]
            q[slot, rows, :] = dot(piece, wq[...]).astype(BF16)
            kv[slot, core, rows, :] = dot(piece, wkv[...]).astype(BF16)
            return carry

        lax.fori_loop(0, blocks, step, 0)
        misc.send(2 + slot, kv.at[slot, core], kv.at[slot, core], at.peer(0, 0, 1))

    def keyval_arrived(slot):
        misc.take(2 + slot, kv.at[slot, 1 - core], at.peer(0, 0, 1))

    def attend(head):
        cols = pl.ds(head * 128, 128)
        for i in range(blocks):
            rows, seen = pl.ds(i * 256, 256), pl.ds(0, (i + 1) * 256)
            weights, norm = softmax_block(q[0, rows, cols], kv[0, 0, seen, :], i * 256)
            att[0, rows, cols] = (dot(weights.astype(BF16), kv[0, 1, seen, :]) / norm).astype(BF16)

    def attend_back(head):
        cols = pl.ds(head * 128, 128)
        for i in range(blocks):
            rows, seen = pl.ds(i * 256, 256), pl.ds(0, (i + 1) * 256)
            q_blk, keys, vals = q[1, rows, cols], kv[1, 0, seen, :], kv[1, 1, seen, :]
            weights, norm = softmax_block(q_blk, keys, i * 256)
            weights = weights / norm
            rounded = weights.astype(BF16)
            att[1, rows, cols] = dot(rounded, vals).astype(BF16)
            d_blk = d_out[rows, cols]
            d_weights = dot(d_blk, vals, ((1,), (1,)))
            delta = jnp.sum(weights * d_weights, axis=-1, keepdims=True)
            d_scores = (weights * (d_weights - delta) * scale).astype(BF16)
            dq[rows, cols] = dot(d_scores, keys).astype(BF16)
            dk[seen, :] += dot(d_scores, q_blk, ((0,), (0,)))
            dv[seen, :] += dot(rounded, d_blk, ((0,), (0,)))

    half = width // 2
    halves = [pl.ds(0, half), pl.ds(half, half)]
    rows_of = Scatter.ROWS // 2
    rs_f = [
        Scatter(at, split, g.at[0], land.at[0], 0, halves[h], rs_send.at[h], rs_recv.at[h])
        for h, split in enumerate((TILT_RIGHT, TILT_LEFT))
    ]
    rs_b = [
        Scatter(at, split, g.at[1], land.at[1], h * rows_of, pl.ds(0, width), rs_send.at[2 + h], rs_recv.at[2 + h])
        for h, split in enumerate((UPPER, LOWER))
    ]

    def produce(dx, buf, first, count, term):
        rows = pl.ds(rs_f[0].block(dx), 256)

        def step(j, carry):
            cols = pl.ds(pl.multiple_of(first + j * 1024, 1024), 1024)
            g[buf, rows, cols] = term(rows, cols).astype(BF16)
            return carry

        lax.fori_loop(0, count // 1024, step, 0)

    def forward_term(rows, cols):
        return dot(att[0, rows, :], wo[:, cols])

    def back_term(rows, cols):
        term = dot(dq[rows, :], wq[cols, :], ((1,), (1,)))
        return term + dot(dkv[rows, :], wkv[cols, :], ((1,), (1,)))

    project(0, 0)
    ag_u.mid2()
    ag_b.mid()
    keyval_arrived(0)
    attend(0)
    ag_u.fin()
    attend(1)
    ag_b.mid2()
    ag_f.move.drain()
    for h, sums in enumerate(rs_f):
        for i, dx in enumerate(Scatter.ORDER):
            produce(dx, 0, h * half, half, forward_term)
            sums.share(dx)
            if i:
                sums.join(Scatter.ORDER[i - 1])
        sums.join(0)

    def cotangent_step(i, carry):
        rows = pl.ds(pl.multiple_of(i * 256, 256), 256)
        d_out[rows, :] = dot(g[1, rows, :], wo[...], ((1,), (1,))).astype(BF16)
        return carry

    lax.fori_loop(0, blocks, cotangent_step, 0)
    ag_b.fin()
    project(2, 1)
    dk[...] = jnp.zeros_like(dk)
    dv[...] = jnp.zeros_like(dv)
    scale = 1.0 / math.sqrt(dk.shape[1])
    rs_f[0].cross()
    keyval_arrived(1)
    attend_back(0)
    rs_f[1].cross()
    attend_back(1)
    even = core == 0
    dkv_send[...] = jnp.where(even, dv[...], dk[...]).astype(BF16)
    misc.send(4, dkv_send, dkv_recv, at.peer(0, 0, 1))
    att_t = att[1].T

    def output_grad_step(j, carry):
        cols = pl.ds(pl.multiple_of(j * 512, 512), 512)
        og[:, cols] = dot(att_t, g[1, :, cols]).astype(BF16)
        return carry

    lax.fori_loop(0, width // 512, output_grad_step, 0)
    og_copy = pltpu.make_async_copy(og, og_out, local_sem.at[5])
    og_copy.start()
    rs_f[0].cross2()
    misc.take(4, dkv_recv, at.peer(0, 0, 1))
    dkv[...] = (jnp.where(even, dk[...], dv[...]) + dkv_recv[...].astype(F32)).astype(BF16)
    ag_u.move.drain()

    for i, dx in enumerate(Scatter.ORDER):
        produce(dx, 1, 0, width, back_term)
        for sums in rs_b:
            sums.share(dx)
        if i:
            for sums in rs_b:
                sums.join(Scatter.ORDER[i - 1])
    for sums in rs_b:
        sums.join(0)
    rs_f[1].cross2()
    rs_b[0].cross()

    for h, sums in enumerate(rs_f):
        sums.total(fwd_rows, inc)
        misc.send(7 + h, fwd_rows.at[:, halves[h]], next_out.at[:, halves[h]], at.relay(1))
    rs_b[1].cross()

    grad_t = jnp.concatenate([dq[...], dkv[...]], axis=1).T

    def weight_grad_step(j, carry):
        cols = pl.ds(pl.multiple_of(j * 512, 512), 512)
        block = dot(grad_t, g[2, :, cols]).astype(BF16).T
        wq[cols, :] = block[:, :256]
        wkv[cols, :] = block[:, 256:]
        return carry

    steps = width // 512
    lax.fori_loop(0, steps // 2, weight_grad_step, 0)
    rs_b[0].cross2()
    lax.fori_loop(steps // 2, steps, weight_grad_step, 0)
    qg_copy = pltpu.make_async_copy(wq, qg_out, local_sem.at[6])
    kg_copy = pltpu.make_async_copy(wkv, kg_out, local_sem.at[7])
    qg_copy.start()
    kg_copy.start()
    rs_b[1].cross2()

    d_gain = jnp.zeros((1, width), F32)
    for i, sums in enumerate(rs_b):
        sums.total(d_rows)
        rows = pl.ds(i * 32, 32)
        d_normed = d_rows[rows, :]
        values = stash[rows, :].astype(F32)
        inverse = inverse_rms(values)
        scaled = d_normed * gain[...]
        inner = jnp.mean(scaled * values, axis=-1, keepdims=True)
        change = inverse * scaled - values * (inverse * inverse * inverse * inner)
        back_rows[rows, :] = (cot[rows, :].astype(F32) + change).astype(BF16)
        misc.send(5 + i, back_rows.at[rows], back_out.at[rows], at.relay(-1))
        d_gain = d_gain + jnp.sum(d_normed * (values * inverse), axis=0, keepdims=True)
    gains = Mover(gs_send, gs_recv)
    piece = width // ranks
    for k in range(ranks):
        gain_send[k] = d_gain[:, k * piece:(k + 1) * piece]
    for k in range(1, ranks):
        there = lax.rem(at.d + k, ranks)
        gains.send(k, gain_send.at[there], gain_recv.at[k], (at.s, there))
    gain_sum = gain_send[at.d]
    for k in range(1, ranks):
        gains.take(k, gain_recv.at[k], (at.s, lax.rem(at.d + k, ranks)))
        gain_sum = gain_sum + gain_recv[k]
    gain_out[...] = gain_sum

    for copy in (og_copy, qg_copy, kg_copy):
        copy.wait()
    for mover in [ag_b.move, gains] + [sums.move for sums in rs_f + rs_b]:
        mover.drain()
    misc.take(1, parkn_out, at.relay(4))
    for i in range(2):
        misc.take(5 + i, back_out.at[pl.ds(i * 32, 32)], at.relay(1))
        misc.take(7 + i, next_out.at[:, halves[i]], at.relay(-1))
    misc.drain()


def deliver(*refs):
    count = (len(refs) - 1) // 3
    sem, held = refs[-1], refs[2 * count:3 * count]
    into = [pltpu.make_async_copy(refs[i], held[i], sem.at[i]) for i in range(count)]
    out = [pltpu.make_async_copy(held[i], refs[count + i], sem.at[count + i]) for i in range(count)]
    for copy in into:
        copy.start()
    for first, second in zip(into, out):
        first.wait()
        second.start()
    for copy in out:
        copy.wait()


def cycle(inc, parked, cot, gain, teacher, language, wq, wkv, wo):
    tokens, width = inc.shape
    ranks = lax.axis_size("dp")
    length = tokens * ranks
    any_spec = pl.BlockSpec(memory_space=pl.ANY)
    vmem_spec = pl.BlockSpec(memory_space=pltpu.VMEM)
    block = jax.ShapeDtypeStruct((tokens, width), BF16)
    shapes = [block, block, block] + [jax.ShapeDtypeStruct(w.shape, BF16) for w in (wq, wkv, wo)]
    heads_width, head_dim = wq.shape[1], wkv.shape[1]
    scratch = [
        pltpu.VMEM((3, length, width), BF16),
        pltpu.VMEM((2, Scatter.ROWS, width), BF16),
        pltpu.VMEM(wq.shape, BF16),
        pltpu.VMEM(wkv.shape, BF16),
        pltpu.VMEM(wo.shape, BF16),
        pltpu.VMEM(wo.shape, BF16),
        pltpu.VMEM((tokens, width), BF16),
        pltpu.VMEM((tokens, width), BF16),
        pltpu.VMEM((tokens, width), BF16),
        pltpu.VMEM((tokens, width), BF16),
        pltpu.VMEM((tokens, width), BF16),
        pltpu.VMEM((tokens, width), F32),
        pltpu.VMEM((2, length, heads_width), BF16),
        pltpu.VMEM((2, 2, length, head_dim), BF16),
        pltpu.VMEM((2, length, heads_width), BF16),
        pltpu.VMEM((length, heads_width), BF16),
        pltpu.VMEM((length, heads_width), BF16),
        pltpu.VMEM((length, head_dim), F32),
        pltpu.VMEM((length, head_dim), F32),
        pltpu.VMEM((length, head_dim), BF16),
        pltpu.VMEM((length, head_dim), BF16),
        pltpu.VMEM((length, head_dim), BF16),
        pltpu.VMEM((ranks, 1, width // ranks), F32),
        pltpu.VMEM((ranks, 1, width // ranks), F32),
        pltpu.SemaphoreType.DMA((3, 34)),
        pltpu.SemaphoreType.DMA((3, 34)),
        pltpu.SemaphoreType.DMA((4, 25)),
        pltpu.SemaphoreType.DMA((4, 25)),
        pltpu.SemaphoreType.DMA((9,)),
        pltpu.SemaphoreType.DMA((9,)),
        pltpu.SemaphoreType.DMA((ranks,)),
        pltpu.SemaphoreType.DMA((ranks,)),
        pltpu.SemaphoreType.DMA((8,)),
    ]
    results = pl.pallas_call(
        kernel,
        out_shape=shapes + [jax.ShapeDtypeStruct((1, width // ranks), F32)],
        in_specs=[any_spec, any_spec, any_spec, vmem_spec, vmem_spec, vmem_spec, any_spec, any_spec, any_spec],
        out_specs=[any_spec] * 6 + [vmem_spec],
        scratch_shapes=scratch,
        compiler_params=pltpu.CompilerParams(
            collective_id=0, has_side_effects=True, vmem_limit_bytes=62 * 2**20
        ),
        cost_estimate=pl.CostEstimate(flops=24 * 10**9, bytes_accessed=2 * 10**7, transcendentals=4 * 10**6),
        name="relay_cycle",
    )(inc, parked, cot, gain, teacher, language, wq, wkv, wo)
    delivered = pl.pallas_call(
        deliver,
        out_shape=shapes,
        in_specs=[any_spec] * 6,
        out_specs=[any_spec] * 6,
        scratch_shapes=[pltpu.VMEM(shape.shape, BF16) for shape in shapes] + [pltpu.SemaphoreType.DMA((12,))],
        compiler_params=pltpu.CompilerParams(vmem_limit_bytes=62 * 2**20),
        name="deliver",
    )(*results[:6])
    return (*delivered, results[6])


def body(
    incoming,
    parked,
    cotangent,
    norm_gain,
    query_weight,
    keyval_weight,
    output_weight,
    teacher_id,
    language_id,
):
    results = cycle(
        incoming[0], parked[0], cotangent[0], norm_gain, teacher_id[None], language_id[None],
        query_weight[0], keyval_weight[0], output_weight[0],
    )
    return tuple(item[None] for item in results[:6]) + (results[6],)


def solution(mesh):
    return jax.shard_map(
        body,
        mesh=mesh,
        in_specs=(
            P("section", "dp", None),
            P("section", "dp", None),
            P("section", "dp", None),
            P("section", None),
            P("section", None, "dp"),
            P("section", None, "dp"),
            P("section", "dp", None),
            P("dp"),
            P("dp"),
        ),
        out_specs=(
            P("section", "dp", None),
            P("section", "dp", None),
            P("section", "dp", None),
            P("section", None, "dp"),
            P("section", None, "dp"),
            P("section", "dp", None),
            P("section", "dp"),
        ),
        check_vma=False,
    )
```

time: 212 us -> 200 us (0.943)
  Pallas kernels: 187 us -> 199 us
  local copies, waits for them, and re-layouts: 11.6 us -> 0.57 us
  waiting for transfers between devices: 5.85 us -> 0 us
  starting transfers between devices: 4.89 us -> 0 us
    pallas_call x1 -> x2, Pallas kernels: 187 us -> 199 us  [the longest x1 193 us: cycle(): pl.pallas_call(kernel, out_shape=shapes + [jax.ShapeDtypeStruct((1, width...]
    unnamed x12 -> x3, local copies, waits for them, and re-layouts: 10.9 us -> 0.57 us
    all_to_all x1 -> x0, waiting for transfers between devices: 5.85 us -> none  [body(): parts = lax.all_to_all(d_gain.reshape(ranks, -1), 'dp', 0, 0)]
    all_to_all x1 -> x0, starting transfers between devices: 4.89 us -> none  [body(): parts = lax.all_to_all(d_gain.reshape(ranks, -1), 'dp', 0, 0)]
  transfers between devices with their start and end apart: 1 -> 0, of which waited for: 1 -> 0; matrix products, arithmetic and copies ran while one was open for 0% -> 0% of each run, Pallas kernels for 0% -> 0%
where the time goes in v2:
time: 200 us
  Pallas kernels  199 us (100%)
    pallas_call x1, Pallas kernels, cycle(): pl.pallas_call(kernel, out_shape=shapes + [jax.ShapeDtypeStruct((1, width...  193 us
    pallas_call x1, Pallas kernels, cycle(): pl.pallas_call(deliver, out_shape=shapes, in_specs=[any_spec] * 6, out_sp...  5.93 us

profile of v2, /device:TPU:1, one launch (start us, length us, event | category | flops | bytes accessed | tf_op | source)
XLA Modules:
  0.0 199.8 jit_solution(699691523525011359)
XLA Ops:
  0.6 192.7 %relay_cycle.1 = (bf16[64,4096]{1,0:T(8,128)(2,1)}, bf16[64,4096]{1,0:T(8,128)(2,1)}, bf16[64,4096]{1,0:T(8,128)(2,1)}, bf16[4096,256]{1,0:T(8,128)(2,1)}, bf16[...) custom-call(bf16[64,4096]{1,0:T(8,128)(2,1)} %bitcast.20, bf16[64,4096]{1,0:T(8,128)(2,1)} %bitcast.21, ...), custom_call_target="tpu_custom_call" | custom-call | flops 24000000000 | bytes 20000000 | tf_op jit(solution)/shard_map/relay_cycle/pallas_call | solution.py:584
  193.3 0.0 copy-start
  193.3 5.9 %deliver.1 = (bf16[64,4096]{1,0:T(8,128)(2,1)}, bf16[64,4096]{1,0:T(8,128)(2,1)}, bf16[64,4096]{1,0:T(8,128)(2,1)}, bf16[4096,256]{1,0:T(8,128)(2,1)}, bf16[4096...) custom-call(bf16[64,4096]{1,0:T(8,128)(2,1)} %get-tuple-element.20.refs_0_, bf16[64,4096]{1,0:T(8,128)(2,1)} %get-tuple-element.21.refs_1_, ...), custom_call_target="tpu_custom_call" | custom-call | tf_op jit(solution)/shard_map/deliver/pallas_call | solution.py:596
  199.2 0.0 copy-done
  199.3 0.6 copy.17
Async XLA Ops:
  193.3 6.0 %copy-start = (f32[1,256]{1,0:T(1,128)S(1)}, f32[1,256]{1,0:T(1,128)}, u32[]{:S(2)}) copy-start(f32[1,256]{1,0:T(1,128)} %get-tuple-element.46) | copy-start | bytes 3076

commit v3 on v2

--- a/solution.py
+++ b/solution.py
@@ -36,6 +36,20 @@
 TILT_LEFT = Split(0, 0, 16, 48, 64)
 UPPER = Split(0, 16, 16, 16, 32)
 LOWER = Split(32, 32, 48, 64, 64)
+
+
+SEQUENCE = [
+    "fs", "fm1", "fm2", "bs", "ffin1", "fm3", "fn1", "fn2", "us", "bm1", "ffin2", "ffin3", "um1", "bm3",
+    "bm2", "projf", "att0", "att1", "pf00", "bfin1", "bn1", "um2", "rf0j0", "pf02", "un1", "pf01", "pf10",
+    "um3", "rf0j2", "pf1-1", "pf11", "bn2", "pf0-1", "ufin1", "rf1j0", "pf12", "bfin2", "un2", "rf0j-1",
+    "bfin3", "projb", "rf1j1", "rf0j1", "ufin2", "rf1j2", "rf0B", "rf1j-1", "ufin3", "cot", "rf1B", "rf0A",
+    "back0", "rf0D", "rf0C", "back1", "rf0E", "dkv", "rf1D", "og", "rf0T", "dkvt", "pb2", "pb-1", "rf1C",
+    "rb0j2", "pb1", "rb0j-1", "rf1A", "pb0", "rb0j1", "rb0B", "rb0j0", "rb1j0", "rb0A", "g1", "rb1j2", "rb0C",
+    "rb1j-1", "rb1A", "rb1j1", "rb1B", "rf1E", "g0", "rb0D", "rb0E", "rb1D", "g3", "rb1E", "rf1T", "rb0T",
+    "g2", "rb1C", "rb1T",
+]
+GATHER_SPLITS = (EVEN, EVEN, TILT_LEFT)
+SCATTER_SPLITS = (TILT_LEFT, EVEN)
 
 
 class Place:
@@ -118,47 +132,50 @@
         self.sib(own, self.split.A)
         self.sib(own, self.split.B)
 
-    def mid(self):
-        right, left, up = (1, 0), (-1, 0), (0, 1)
-        self.got(13, up, self.split.B)
-        self.go(2, up, self.split.B, right)
-        self.go(8, up, self.split.B, left)
-        self.got(0, left, self.split.A)
-        self.go(3, left, self.split.A0, right)
-        self.go(14, left, self.split.A, up)
-        self.got(6, right, self.split.A)
-        self.go(9, right, self.split.A1, left)
-        self.go(15, right, self.split.A, up)
-        self.sib(up, self.split.B)
-        self.sib(left, self.split.A)
-        self.sib(right, self.split.A)
-        self.got(1, left, self.split.B)
-        self.go(4, left, self.split.B0, right)
-        self.got(7, right, self.split.B)
-        self.go(10, right, self.split.B1, left)
-        self.sib(left, self.split.B)
-        self.sib(right, self.split.B)
-
-    def mid2(self):
-        right, left, up = (1, 0), (-1, 0), (0, 1)
+    def m1(self):
+        self.got(13, (0, 1), self.split.B)
+        self.go(2, (0, 1), self.split.B, (1, 0))
+        self.go(8, (0, 1), self.split.B, (-1, 0))
+        self.sib((0, 1), self.split.B)
+
+    def m2(self):
+        self.got(0, (-1, 0), self.split.A)
+        self.go(3, (-1, 0), self.split.A0, (1, 0))
+        self.go(14, (-1, 0), self.split.A, (0, 1))
+        self.got(6, (1, 0), self.split.A)
+        self.go(9, (1, 0), self.split.A1, (-1, 0))
+        self.go(15, (1, 0), self.split.A, (0, 1))
+        self.sib((-1, 0), self.split.A)
+        self.sib((1, 0), self.split.A)
+
+    def m3(self):
+        self.got(1, (-1, 0), self.split.B)
+        self.go(4, (-1, 0), self.split.B0, (1, 0))
+        self.got(7, (1, 0), self.split.B)
+        self.go(10, (1, 0), self.split.B1, (-1, 0))
+        self.sib((-1, 0), self.split.B)
+        self.sib((1, 0), self.split.B)
+
+    def n1(self):
         self.got(2, (-1, 1), self.split.B)
-        self.go(5, (-1, 1), self.split.B0, right)
+        self.go(5, (-1, 1), self.split.B0, (1, 0))
         self.got(8, (1, 1), self.split.B)
-        self.go(11, (1, 1), self.split.B1, left)
+        self.go(11, (1, 1), self.split.B1, (-1, 0))
         self.sib((-1, 1), self.split.B)
         self.sib((1, 1), self.split.B)
+
+    def n2(self):
         self.got(3, (2, 0), self.split.A0)
         self.got(9, (2, 0), self.split.A1)
-        self.go(16, (2, 0), self.split.A, up)
+        self.go(16, (2, 0), self.split.A, (0, 1))
         self.sib((2, 0), self.split.A)
 
-    def fin(self):
-        self.got(12, (0, 1), self.split.A)
-        self.sib((0, 1), self.split.A)
-        self.got(14, (-1, 1), self.split.A)
-        self.sib((-1, 1), self.split.A)
-        self.got(15, (1, 1), self.split.A)
-        self.sib((1, 1), self.split.A)
+    def fin1(self):
+        for key, where in ((12, (0, 1)), (14, (-1, 1)), (15, (1, 1))):
+            self.got(key, where, self.split.A)
+            self.sib(where, self.split.A)
+
+    def fin2(self):
         self.got(4, (2, 0), self.split.B0)
         self.got(10, (2, 0), self.split.B1)
         self.sib((2, 0), self.split.B)
@@ -167,6 +184,8 @@
         self.sib((2, 1), self.split.B)
         self.got(16, (2, 1), self.split.A)
         self.sib((2, 1), self.split.A)
+
+    def fin3(self):
         for i, where in enumerate(PLACES):
             for j, part in enumerate((self.split.A, self.split.B)):
                 self.move.take(18 + 2 * i + j, self.buf.at[self.at.row(*where, part, 1)], self.at.peer(0, 0, 1))
@@ -221,31 +240,35 @@
         else:
             self.go({-1: 13, 1: 14, 0: 15}[dx], (dx, 1), self.split.A, up)
 
-    def cross(self):
-        right, left = (1, 0), (-1, 0)
+    def cross_a(self):
         self.add(12, (2, 0), self.split.A)
-        self.go(2, (2, 0), self.split.A0, left)
-        self.go(8, (2, 0), self.split.A1, right)
+        self.go(2, (2, 0), self.split.A0, (-1, 0))
+        self.go(8, (2, 0), self.split.A1, (1, 0))
+
+    def cross_b(self):
         self.add(0, (-1, 1), self.split.B0)
-        self.go(3, (-1, 1), self.split.B, left)
+        self.go(3, (-1, 1), self.split.B, (-1, 0))
         self.add(6, (1, 1), self.split.B1)
-        self.go(9, (1, 1), self.split.B, right)
+        self.go(9, (1, 1), self.split.B, (1, 0))
+
+    def cross_c(self):
         self.add(1, (-1, 0), self.split.B0)
-        self.go(4, (-1, 0), self.split.B, left)
+        self.go(4, (-1, 0), self.split.B, (-1, 0))
         self.add(7, (1, 0), self.split.B1)
-        self.go(10, (1, 0), self.split.B, right)
-
-    def cross2(self):
-        right, left, up = (1, 0), (-1, 0), (0, 1)
+        self.go(10, (1, 0), self.split.B, (1, 0))
+
+    def cross_d(self):
         self.add(3, (0, 1), self.split.B)
         self.add(9, (0, 1), self.split.B)
-        self.go(16, (0, 1), self.split.B, up)
+        self.go(16, (0, 1), self.split.B, (0, 1))
+
+    def cross_e(self):
         self.add(13, (-1, 0), self.split.A)
         self.add(2, (-1, 0), self.split.A0)
-        self.go(5, (-1, 0), self.split.A, left)
+        self.go(5, (-1, 0), self.split.A, (-1, 0))
         self.add(14, (1, 0), self.split.A)
         self.add(8, (1, 0), self.split.A1)
-        self.go(11, (1, 0), self.split.A, right)
+        self.go(11, (1, 0), self.split.A, (1, 0))
 
     def total(self, out, start=None):
         for part, keys in ((self.split.A, (15, 5, 11)), (self.split.B, (4, 10, 16))):
@@ -314,25 +337,32 @@
     pl.semaphore_wait(barrier, len(peers))
     misc = Mover(misc_send, misc_recv)
     misc.send(0, parked, stash, at.relay(4))
-    splits = (TILT_LEFT, EVEN, TILT_RIGHT)
-    ag_f, ag_u, ag_b = [Gather(at, splits[i], g.at[i], ag_send.at[i], ag_recv.at[i]) for i in range(3)]
-    ag_f.start()
-    loads[1].wait()
-    cot[...] = (cot[...].astype(F32) * weight).astype(BF16)
-    g[1, own, :] = cot[...]
-    ag_u.start()
-    misc.send(1, inc, parkn_out, at.relay(4))
-    ag_f.mid()
-    misc.take(0, stash, at.relay(4))
-    g[2, own, :] = normalized(stash)
-    ag_b.start()
-    ag_f.mid2()
-    ag_u.mid()
-    ag_f.fin()
-    for load in loads[2:]:
-        load.wait()
+    ag = {
+        name: Gather(at, split, g.at[i], ag_send.at[i], ag_recv.at[i])
+        for i, (name, split) in enumerate(zip("fub", GATHER_SPLITS))
+    }
+    loaded = set()
+
+    def loads_done(*names):
+        for name in names:
+            if name not in loaded:
+                loaded.add(name)
+                loads[name].wait()
+
+    def start_u():
+        loads_done(1)
+        cot[...] = (cot[...].astype(F32) * weight).astype(BF16)
+        g[1, own, :] = cot[...]
+        ag["u"].start()
+
+    def start_b():
+        misc.take(0, stash, at.relay(4))
+        g[2, own, :] = normalized(stash)
+        ag["b"].start()
 
     def project(source, slot):
+        loads_done(2, 3)
+
         def step(i, carry):
             rows = pl.ds(pl.multiple_of(i * 256, 256), 256)
             piece = g[source, rows, :]
@@ -375,7 +405,7 @@
     rows_of = Scatter.ROWS // 2
     rs_f = [
         Scatter(at, split, g.at[0], land.at[0], 0, halves[h], rs_send.at[h], rs_recv.at[h])
-        for h, split in enumerate((TILT_RIGHT, TILT_LEFT))
+        for h, split in enumerate(SCATTER_SPLITS)
     ]
     rs_b = [
         Scatter(at, split, g.at[1], land.at[1], h * rows_of, pl.ds(0, width), rs_send.at[2 + h], rs_recv.at[2 + h])
@@ -399,97 +429,90 @@
         term = dot(dq[rows, :], wq[cols, :], ((1,), (1,)))
         return term + dot(dkv[rows, :], wkv[cols, :], ((1,), (1,)))
 
-    project(0, 0)
-    ag_u.mid2()
-    ag_b.mid()
-    keyval_arrived(0)
-    attend(0)
-    ag_u.fin()
-    attend(1)
-    ag_b.mid2()
-    ag_f.move.drain()
-    for h, sums in enumerate(rs_f):
-        for i, dx in enumerate(Scatter.ORDER):
-            produce(dx, 0, h * half, half, forward_term)
-            sums.share(dx)
-            if i:
-                sums.join(Scatter.ORDER[i - 1])
-        sums.join(0)
-
-    def cotangent_step(i, carry):
-        rows = pl.ds(pl.multiple_of(i * 256, 256), 256)
-        d_out[rows, :] = dot(g[1, rows, :], wo[...], ((1,), (1,))).astype(BF16)
-        return carry
-
-    lax.fori_loop(0, blocks, cotangent_step, 0)
-    ag_b.fin()
-    project(2, 1)
-    dk[...] = jnp.zeros_like(dk)
-    dv[...] = jnp.zeros_like(dv)
+    def cotangent():
+        loads_done(4)
+
+        def step(i, carry):
+            rows = pl.ds(pl.multiple_of(i * 256, 256), 256)
+            d_out[rows, :] = dot(g[1, rows, :], wo[...], ((1,), (1,))).astype(BF16)
+            return carry
+
+        lax.fori_loop(0, blocks, step, 0)
+
+    arrived = set()
+
+    def once(key, act):
+        if key not in arrived:
+            arrived.add(key)
+            act()
+
+    def attend_forward(head):
+        once("keyval f", lambda: keyval_arrived(0))
+        attend(head)
+
+    def attend_backward(head):
+        if head == 0:
+            dk[...] = jnp.zeros_like(dk)
+            dv[...] = jnp.zeros_like(dv)
+            keyval_arrived(1)
+        attend_back(head)
+
     scale = 1.0 / math.sqrt(dk.shape[1])
-    rs_f[0].cross()
-    keyval_arrived(1)
-    attend_back(0)
-    rs_f[1].cross()
-    attend_back(1)
     even = core == 0
-    dkv_send[...] = jnp.where(even, dv[...], dk[...]).astype(BF16)
-    misc.send(4, dkv_send, dkv_recv, at.peer(0, 0, 1))
-    att_t = att[1].T
-
-    def output_grad_step(j, carry):
-        cols = pl.ds(pl.multiple_of(j * 512, 512), 512)
-        og[:, cols] = dot(att_t, g[1, :, cols]).astype(BF16)
-        return carry
-
-    lax.fori_loop(0, width // 512, output_grad_step, 0)
-    og_copy = pltpu.make_async_copy(og, og_out, local_sem.at[5])
-    og_copy.start()
-    rs_f[0].cross2()
-    misc.take(4, dkv_recv, at.peer(0, 0, 1))
-    dkv[...] = (jnp.where(even, dk[...], dv[...]) + dkv_recv[...].astype(F32)).astype(BF16)
-    ag_u.move.drain()
-
-    for i, dx in enumerate(Scatter.ORDER):
+
+    def swap_keyval():
+        dkv_send[...] = jnp.where(even, dv[...], dk[...]).astype(BF16)
+        misc.send(4, dkv_send, dkv_recv, at.peer(0, 0, 1))
+
+    def take_keyval():
+        misc.take(4, dkv_recv, at.peer(0, 0, 1))
+        dkv[...] = (jnp.where(even, dk[...], dv[...]) + dkv_recv[...].astype(F32)).astype(BF16)
+
+    def output_grad():
+        att_t = att[1].T
+
+        def step(j, carry):
+            cols = pl.ds(pl.multiple_of(j * 512, 512), 512)
+            og[:, cols] = dot(att_t, g[1, :, cols]).astype(BF16)
+            return carry
+
+        lax.fori_loop(0, width // 512, step, 0)
+        copies[0].start()
+
+    def forward_block(h, dx):
+        once("drain f", ag["f"].move.drain)
+        loads_done(4)
+        produce(dx, 0, h * half, half, forward_term)
+        rs_f[h].share(dx)
+
+    def back_block(dx):
+        once("drain u", ag["u"].move.drain)
         produce(dx, 1, 0, width, back_term)
         for sums in rs_b:
             sums.share(dx)
-        if i:
-            for sums in rs_b:
-                sums.join(Scatter.ORDER[i - 1])
-    for sums in rs_b:
-        sums.join(0)
-    rs_f[1].cross2()
-    rs_b[0].cross()
-
-    for h, sums in enumerate(rs_f):
-        sums.total(fwd_rows, inc)
+
+    def weight_grads(quarter):
+        grad_t = jnp.concatenate([dq[...], dkv[...]], axis=1).T
+
+        def step(j, carry):
+            cols = pl.ds(pl.multiple_of(j * 512, 512), 512)
+            block = dot(grad_t, g[2, :, cols]).astype(BF16).T
+            wq[cols, :] = block[:, :256]
+            wkv[cols, :] = block[:, 256:]
+            return carry
+
+        steps = width // 2048
+        lax.fori_loop(quarter * steps, (quarter + 1) * steps, step, 0)
+
+    def finish_forward(h):
+        rs_f[h].total(fwd_rows, inc)
         misc.send(7 + h, fwd_rows.at[:, halves[h]], next_out.at[:, halves[h]], at.relay(1))
-    rs_b[1].cross()
-
-    grad_t = jnp.concatenate([dq[...], dkv[...]], axis=1).T
-
-    def weight_grad_step(j, carry):
-        cols = pl.ds(pl.multiple_of(j * 512, 512), 512)
-        block = dot(grad_t, g[2, :, cols]).astype(BF16).T
-        wq[cols, :] = block[:, :256]
-        wkv[cols, :] = block[:, 256:]
-        return carry
-
-    steps = width // 512
-    lax.fori_loop(0, steps // 2, weight_grad_step, 0)
-    rs_b[0].cross2()
-    lax.fori_loop(steps // 2, steps, weight_grad_step, 0)
-    qg_copy = pltpu.make_async_copy(wq, qg_out, local_sem.at[6])
-    kg_copy = pltpu.make_async_copy(wkv, kg_out, local_sem.at[7])
-    qg_copy.start()
-    kg_copy.start()
-    rs_b[1].cross2()
-
-    d_gain = jnp.zeros((1, width), F32)
-    for i, sums in enumerate(rs_b):
-        sums.total(d_rows)
-        rows = pl.ds(i * 32, 32)
+
+    gain_parts = []
+
+    def finish_back(h):
+        rs_b[h].total(d_rows)
+        rows = pl.ds(h * 32, 32)
         d_normed = d_rows[rows, :]
         values = stash[rows, :].astype(F32)
         inverse = inverse_rms(values)
@@ -497,24 +520,64 @@
         inner = jnp.mean(scaled * values, axis=-1, keepdims=True)
         change = inverse * scaled - values * (inverse * inverse * inverse * inner)
         back_rows[rows, :] = (cot[rows, :].astype(F32) + change).astype(BF16)
-        misc.send(5 + i, back_rows.at[rows], back_out.at[rows], at.relay(-1))
-        d_gain = d_gain + jnp.sum(d_normed * (values * inverse), axis=0, keepdims=True)
+        misc.send(5 + h, back_rows.at[rows], back_out.at[rows], at.relay(-1))
+        gain_parts.append(jnp.sum(d_normed * (values * inverse), axis=0, keepdims=True))
+        if len(gain_parts) == 2:
+            d_gain = gain_parts[0] + gain_parts[1]
+            for k in range(ranks):
+                gain_send[k] = d_gain[:, k * piece:(k + 1) * piece]
+            for k in range(1, ranks):
+                there = lax.rem(at.d + k, ranks)
+                gains.send(k, gain_send.at[there], gain_recv.at[k], (at.s, there))
+
     gains = Mover(gs_send, gs_recv)
     piece = width // ranks
-    for k in range(ranks):
-        gain_send[k] = d_gain[:, k * piece:(k + 1) * piece]
-    for k in range(1, ranks):
-        there = lax.rem(at.d + k, ranks)
-        gains.send(k, gain_send.at[there], gain_recv.at[k], (at.s, there))
+    copies = [
+        pltpu.make_async_copy(src, dst, local_sem.at[5 + i])
+        for i, (src, dst) in enumerate(((og, og_out), (wq, qg_out), (wkv, kg_out)))
+    ]
+
+    steps = {
+        "fs": ag["f"].start, "us": start_u, "bs": start_b,
+        "projf": lambda: project(0, 0), "projb": lambda: project(2, 1), "cot": cotangent,
+        "dkv": swap_keyval, "dkvt": take_keyval, "og": output_grad,
+    }
+    for name, gather in ag.items():
+        for stage in ("m1", "m2", "m3", "n1", "n2", "fin1", "fin2", "fin3"):
+            steps[name + stage] = getattr(gather, stage)
+    for dx in Scatter.ORDER:
+        steps[f"pb{dx}"] = functools.partial(back_block, dx)
+    for quarter in range(4):
+        steps[f"g{quarter}"] = functools.partial(weight_grads, quarter)
+    for h in range(2):
+        steps[f"att{h}"] = functools.partial(attend_forward, h)
+        steps[f"back{h}"] = functools.partial(attend_backward, h)
+        for dx in Scatter.ORDER:
+            steps[f"pf{h}{dx}"] = functools.partial(forward_block, h, dx)
+        for name, sums in ((f"rf{h}", rs_f[h]), (f"rb{h}", rs_b[h])):
+            for dx in Scatter.ORDER:
+                steps[f"{name}j{dx}"] = functools.partial(sums.join, dx)
+            for stage in "ABCDE":
+                steps[name + stage] = getattr(sums, "cross_" + stage.lower())
+        steps[f"rf{h}T"] = functools.partial(finish_forward, h)
+        steps[f"rb{h}T"] = functools.partial(finish_back, h)
+
+    for i, name in enumerate(SEQUENCE):
+        if i == 1:
+            misc.send(1, inc, parkn_out, at.relay(4))
+        steps[name]()
+    copies[1].start()
+    copies[2].start()
+
     gain_sum = gain_send[at.d]
     for k in range(1, ranks):
         gains.take(k, gain_recv.at[k], (at.s, lax.rem(at.d + k, ranks)))
         gain_sum = gain_sum + gain_recv[k]
     gain_out[...] = gain_sum
 
-    for copy in (og_copy, qg_copy, kg_copy):
+    for copy in copies:
         copy.wait()
-    for mover in [ag_b.move, gains] + [sums.move for sums in rs_f + rs_b]:
+    for mover in [ag["b"].move, gains] + [sums.move for sums in rs_f + rs_b]:
         mover.drain()
     misc.take(1, parkn_out, at.relay(4))
     for i in range(2):

time: 200 us -> 179 us (0.90)
  Pallas kernels: 199 us -> 178 us
    pallas_call x1, Pallas kernels: 193 us -> 172 us  [cycle(): pl.pallas_call(kernel, out_shape=shapes + [jax.ShapeDtypeStruct((1, width...]
where the time goes in v3:
time: 179 us
  Pallas kernels  178 us (99%)
    pallas_call x1, Pallas kernels, cycle(): pl.pallas_call(kernel, out_shape=shapes + [jax.ShapeDtypeStruct((1, width...  172 us
    pallas_call x1, Pallas kernels, cycle(): pl.pallas_call(deliver, out_shape=shapes, in_specs=[any_spec] * 6, out_sp...  5.93 us

profile of v3, /device:TPU:1, one launch (start us, length us, event | category | flops | bytes accessed | tf_op | source)
XLA Modules:
  0.0 179.2 jit_solution(6529711081294413626)
XLA Ops:
  0.6 172.1 %relay_cycle.1 = (bf16[64,4096]{1,0:T(8,128)(2,1)}, bf16[64,4096]{1,0:T(8,128)(2,1)}, bf16[64,4096]{1,0:T(8,128)(2,1)}, bf16[4096,256]{1,0:T(8,128)(2,1)}, bf16[...) custom-call(bf16[64,4096]{1,0:T(8,128)(2,1)} %bitcast.20, bf16[64,4096]{1,0:T(8,128)(2,1)} %bitcast.21, ...), custom_call_target="tpu_custom_call" | custom-call | flops 24000000000 | bytes 20000000 | tf_op jit(solution)/shard_map/relay_cycle/pallas_call | solution.py:647
  172.7 0.0 copy-start
  172.7 5.9 %deliver.1 = (bf16[64,4096]{1,0:T(8,128)(2,1)}, bf16[64,4096]{1,0:T(8,128)(2,1)}, bf16[64,4096]{1,0:T(8,128)(2,1)}, bf16[4096,256]{1,0:T(8,128)(2,1)}, bf16[4096...) custom-call(bf16[64,4096]{1,0:T(8,128)(2,1)} %get-tuple-element.20.refs_0_, bf16[64,4096]{1,0:T(8,128)(2,1)} %get-tuple-element.21.refs_1_, ...), custom_call_target="tpu_custom_call" | custom-call | tf_op jit(solution)/shard_map/deliver/pallas_call | solution.py:659
  178.7 0.0 copy-done
  178.7 0.6 copy.17
Async XLA Ops:
  172.7 6.0 %copy-start = (f32[1,256]{1,0:T(1,128)S(1)}, f32[1,256]{1,0:T(1,128)}, u32[]{:S(2)}) copy-start(f32[1,256]{1,0:T(1,128)} %get-tuple-element.46) | copy-start | bytes 3076

commit v4 on v3

--- a/solution.py
+++ b/solution.py
@@ -589,8 +589,13 @@
 def deliver(*refs):
     count = (len(refs) - 1) // 3
     sem, held = refs[-1], refs[2 * count:3 * count]
-    into = [pltpu.make_async_copy(refs[i], held[i], sem.at[i]) for i in range(count)]
-    out = [pltpu.make_async_copy(held[i], refs[count + i], sem.at[count + i]) for i in range(count)]
+    into, out = [], []
+    for i in range(count):
+        size = held[i].shape[0] // 4
+        for part in range(4):
+            rows, key = pl.ds(part * size, size), 4 * i + part
+            into.append(pltpu.make_async_copy(refs[i].at[rows], held[i].at[rows], sem.at[0, key]))
+            out.append(pltpu.make_async_copy(held[i].at[rows], refs[count + i].at[rows], sem.at[1, key]))
     for copy in into:
         copy.start()
     for first, second in zip(into, out):
@@ -661,7 +666,7 @@
         out_shape=shapes,
         in_specs=[any_spec] * 6,
         out_specs=[any_spec] * 6,
-        scratch_shapes=[pltpu.VMEM(shape.shape, BF16) for shape in shapes] + [pltpu.SemaphoreType.DMA((12,))],
+        scratch_shapes=[pltpu.VMEM(shape.shape, BF16) for shape in shapes] + [pltpu.SemaphoreType.DMA((2, 24))],
         compiler_params=pltpu.CompilerParams(vmem_limit_bytes=62 * 2**20),
         name="deliver",
     )(*results[:6])

time: 179 us -> 180 us (level)
  no operation moved by 1% of the time
where the time goes in v4:
time: 180 us; the launch traced here: 179 us
  Pallas kernels  178 us (99%)
    pallas_call x1, Pallas kernels, cycle(): pl.pallas_call(kernel, out_shape=shapes + [jax.ShapeDtypeStruct((1, width...  172 us
    pallas_call x1, Pallas kernels, cycle(): pl.pallas_call(deliver, out_shape=shapes, in_specs=[any_spec] * 6, out_sp...  6.1 us

profile of v4, /device:TPU:1, one launch (start us, length us, event | category | flops | bytes accessed | tf_op | source)
XLA Modules:
  0.0 179.4 jit_solution(10252414949080732941)
XLA Ops:
  0.6 172.1 %relay_cycle.1 = (bf16[64,4096]{1,0:T(8,128)(2,1)}, bf16[64,4096]{1,0:T(8,128)(2,1)}, bf16[64,4096]{1,0:T(8,128)(2,1)}, bf16[4096,256]{1,0:T(8,128)(2,1)}, bf16[...) custom-call(bf16[64,4096]{1,0:T(8,128)(2,1)} %bitcast.20, bf16[64,4096]{1,0:T(8,128)(2,1)} %bitcast.21, ...), custom_call_target="tpu_custom_call" | custom-call | flops 24000000000 | bytes 20000000 | tf_op jit(solution)/shard_map/relay_cycle/pallas_call | solution.py:652
  172.7 0.0 copy-start
  172.7 6.1 %deliver.1 = (bf16[64,4096]{1,0:T(8,128)(2,1)}, bf16[64,4096]{1,0:T(8,128)(2,1)}, bf16[64,4096]{1,0:T(8,128)(2,1)}, bf16[4096,256]{1,0:T(8,128)(2,1)}, bf16[4096...) custom-call(bf16[64,4096]{1,0:T(8,128)(2,1)} %get-tuple-element.20.refs_0_, bf16[64,4096]{1,0:T(8,128)(2,1)} %get-tuple-element.21.refs_1_, ...), custom_call_target="tpu_custom_call" | custom-call | tf_op jit(solution)/shard_map/deliver/pallas_call | solution.py:664
  178.8 0.0 copy-done
  178.9 0.6 copy.17
Async XLA Ops:
  172.7 6.1 %copy-start = (f32[1,256]{1,0:T(1,128)S(1)}, f32[1,256]{1,0:T(1,128)}, u32[]{:S(2)}) copy-start(f32[1,256]{1,0:T(1,128)} %get-tuple-element.46) | copy-start | bytes 3076
